TPU v7x, 1024 devices: a whole 4x8x16 slice. The times are simulated.
1024 devices in a mesh: group: 64 (over x, z), shard: 16 (over y, core).
Axes of the slice: x: 4, y: 8, z: 16, core: 2. Of those that a mesh axis runs over, the one named last changes fastest.
Arguments:
- embeddings: bfloat16 [524288, 768], P(('group', 'shard')), may hold values from -1000 to 1000
- cluster_id: int32 [524288], P(('group', 'shard')), may hold values from 0 to 127, as said below
- row_index: int32 [524288], P(('group', 'shard')), may hold values from 0 to 524287, each once
Outputs:
- best: float32 [524288], P(('group', 'shard'))
Inputs may be any that keep to these rules, and one draw needn't show every extreme that they name: `cluster_id`: cluster c of a group is owned by shard index c // 8. The rows of one device name clusters of one owner at most 64 times, and in every group one owner is named exactly 64 times by the rows of each device of the group.
All inputs are finite; a program needn't handle non-finite values.
Results may differ from a plain program's by a relative error of at most 0.00059.
Values may be sent and summed in bfloat16 or wider, within the bound.
No kernel may reach another device: no remote copies, remote signals or barrier semaphores. Data moves between devices by JAX's collectives and lax.ppermute only.
A program may use at most 64 MiB of HBM per device.

v0:
```python
import functools

import jax
import jax.numpy as jnp
from jax import lax
from jax.experimental import pallas as pl
from jax.experimental.pallas import tpu as pltpu
from jax.sharding import Mesh, PartitionSpec as P

F32 = jnp.float32
BF16 = jnp.bfloat16
FEAT = 768
BLK = 64
NBLK = FEAT // BLK
PANELS = BLK // 8
LANES = 128
WHOLE = [(i, j) for i in range(NBLK) for j in range((i + 1) // 2)]
PAIRED = [(i, i + 2) for i in range(0, NBLK, 4)]
TILES = len(WHOLE) + len(PAIRED) + 1
HALF = TILES // 2 * BLK
WIDE = FEAT + LANES
CAP = 64
CL_OWN = 8
INDEX_SPAN = 2**19
PIECES = 2
HIGHEST = lax.Precision.HIGHEST
VM = pl.BlockSpec(memory_space=pltpu.VMEM)
SM = pl.BlockSpec(memory_space=pltpu.SMEM)
ANY = pl.BlockSpec(memory_space=pl.ANY)
PARAMS = pltpu.CompilerParams(vmem_limit_bytes=24 * 2**20)


def nt(a, b, precision=None):
    return lax.dot_general(
        a, b, (((1,), (1,)), ((), ())), precision=precision, preferred_element_type=F32
    )


def nn(a, b, precision=None):
    return lax.dot_general(
        a, b, (((1,), (0,)), ((), ())), precision=precision, preferred_element_type=F32
    )


def split3(x):
    high = x.astype(BF16)
    rest = x - high.astype(F32)
    mid = rest.astype(BF16)
    low = (rest - mid.astype(F32)).astype(BF16)
    return high, mid, low


def moments_kernel(core_ref, x_ref, keep_ref, send_ref, tri_ref, sems):
    def put(tile, value):
        at = BLK * (tile % (TILES // 2))
        tri_ref[tile // (TILES // 2), at : at + BLK, :] = value

    x = x_ref[...]
    sums = nn(jnp.ones((8, x.shape[0]), BF16), x)
    put(
        TILES - 1,
        jnp.concatenate(
            [sums[:, LANES * j : LANES * (j + 1)] for j in range(FEAT // LANES)]
            + [jnp.zeros((BLK - 8 * (FEAT // LANES), LANES), F32)],
            axis=0,
        ),
    )
    halves = {}
    for b in range(FEAT // 256):
        left = x[:, 256 * b : 256 * (b + 1)].T
        wide = nn(left, x[:, : 256 * (b + 1)])
        for i in range(4 * b, 4 * b + 4):
            strip = wide[BLK * (i - 4 * b) : BLK * (i - 4 * b + 1), :]
            for j in range((i + 1) // 2):
                put(WHOLE.index((i, j)), strip[:, LANES * j : LANES * (j + 1)])
            if i % 2 == 0:
                halves[i] = strip[:, BLK * i : BLK * (i + 1)]
    for n, (i, j) in enumerate(PAIRED):
        put(len(WHOLE) + n, jnp.concatenate([halves[i], halves[j]], axis=1))
    core = core_ref[0]
    mine = pltpu.make_async_copy(tri_ref.at[core], keep_ref, sems.at[0])
    other = pltpu.make_async_copy(tri_ref.at[1 - core], send_ref, sems.at[1])
    other.start()
    mine.start()
    other.wait()
    mine.wait()


def moments(core, x):
    half = jax.ShapeDtypeStruct((HALF, LANES), F32)
    return pl.pallas_call(
        moments_kernel,
        out_shape=(half, half),
        in_specs=[SM, VM],
        out_specs=(ANY, ANY),
        scratch_shapes=[pltpu.VMEM((2, HALF, LANES), F32), pltpu.SemaphoreType.DMA((2,))],
        compiler_params=PARAMS,
        name="moments",
    )(core, x)


def pack_kernel(x_ref, cluster_ref, index_ref, rows_ref, slot_ref):
    count = x_ref.shape[0]
    slots = rows_ref.shape[0]
    owners = slots // CAP
    cluster = cluster_ref[...]
    owner = cluster // CL_OWN
    member = lax.broadcasted_iota(jnp.int32, (owners, count), 0) == jnp.broadcast_to(
        owner, (owners, count)
    )
    earlier = lax.broadcasted_iota(jnp.int32, (count, count), 0) < lax.broadcasted_iota(
        jnp.int32, (count, count), 1
    )
    prefix = nn(jnp.where(member, 1.0, 0.0).astype(BF16), jnp.where(earlier, 1.0, 0.0).astype(BF16))
    rank = jnp.sum(jnp.where(member, prefix, 0.0), axis=0, keepdims=True).astype(jnp.int32)
    slot = owner * CAP + rank
    slot_ref[...] = slot
    place = jnp.where(
        lax.broadcasted_iota(jnp.int32, (slots, count), 0) == jnp.broadcast_to(slot, (slots, count)),
        1.0,
        0.0,
    ).astype(BF16)
    rows_ref[:, :FEAT] = nn(place, x_ref[...]).astype(BF16)
    digit = lax.broadcasted_iota(jnp.int32, (LANES, count), 0)
    whole = jnp.broadcast_to(cluster * INDEX_SPAN + index_ref[...], (LANES, count))
    parts = jnp.where(digit < 4, (whole >> (7 * jnp.minimum(digit, 3))) & 127, 1)
    rows_ref[:, FEAT:] = nt(place, parts.astype(F32).astype(BF16)).astype(BF16)


def pack(x, cluster_id, row_index, owners):
    count = x.shape[0]
    slots = owners * CAP
    return pl.pallas_call(
        pack_kernel,
        out_shape=(
            jax.ShapeDtypeStruct((slots, WIDE), BF16),
            jax.ShapeDtypeStruct((1, count), jnp.int32),
        ),
        in_specs=[VM, VM, VM],
        out_specs=(VM, VM),
        compiler_params=PARAMS,
        name="pack_rows",
    )(x, cluster_id.reshape(1, count), row_index.reshape(1, count))


def inverse_factor(block, spot_ref):
    lane = lax.broadcasted_iota(jnp.int32, (8, LANES), 1)
    sub = lax.broadcasted_iota(jnp.int32, (8, LANES), 0)
    wide = jnp.concatenate([block, jnp.zeros((BLK, BLK), F32)], axis=1)
    a = [
        jnp.where(lane < BLK, wide[8 * g : 8 * g + 8], jnp.where(lane == sub + 8 * g + BLK, 1.0, 0.0))
        for g in range(PANELS)
    ]
    out = []

    def row(x, k):
        return jnp.broadcast_to(x[k : k + 1, :], (8, LANES))

    def column(x, k):
        return jnp.broadcast_to(x[:, k : k + 1], (8, LANES))

    for g in range(PANELS):
        d = [column(a[g], 8 * g + k) for k in range(8)]
        m = {h: [column(a[h], 8 * g + k) for k in range(8)] for h in range(g + 1, PANELS)}
        base = 64 * (g % 2)
        for l in range(8):
            spot_ref[base + 8 * l : base + 8 * l + 8, :] = d[l]
        s = {
            (k, l): jnp.broadcast_to(spot_ref[base + 8 * l + k : base + 8 * l + k + 1, :], (8, LANES))
            for k in range(8)
            for l in range(k, 8)
        }
        scale = [None] * 8
        for k in range(0, 8, 2):
            p, q, t = s[k, k], s[k, k + 1], s[k + 1, k + 1]
            det = p * t - q * q
            guess = pl.reciprocal(det, approx=True)
            fix = 2.0 - det * guess
            over = guess * fix
            ua = {l: s[k, l] * t - s[k + 1, l] * q for l in range(k + 2, 8)}
            ub = {l: s[k + 1, l] * p - s[k, l] * q for l in range(k + 2, 8)}
            for l in range(k + 2, 8):
                for n in range(l, 8):
                    num = ua[l] * s[k, n] + ub[l] * s[k + 1, n]
                    s[l, n] = s[l, n] - (num * guess) * fix
            root = lax.rsqrt(p)
            scale[k] = root
            scale[k + 1] = lax.rsqrt(det) * (p * root)
            a0, a1 = row(a[g], k), row(a[g], k + 1)
            va = (a0 * t - a1 * q) * over
            vb = (a1 * p - a0 * q) * over
            sa = {l: ua[l] * over for l in ua}
            sb = {l: ub[l] * over for l in ub}
            ma = jnp.where(sub > k + 1, d[k], 0.0)
            mb = jnp.where(sub > k + 1, d[k + 1], 0.0)
            for l in range(k + 2, 8):
                d[l] = d[l] - (ma * sa[l] + mb * sb[l])
            low = jnp.where(sub == k + 1, q * (root * root), 0.0)
            a[g] = a[g] - (ma * va + mb * vb) - low * a0
            for h in range(g + 1, PANELS):
                ha, hb = m[h][k], m[h][k + 1]
                for l in range(k + 2, 8):
                    m[h][l] = m[h][l] - (ha * sa[l] + hb * sb[l])
                a[h] = a[h] - (ha * va + hb * vb)
        scales = scale[0]
        for k in range(1, 8):
            scales = jnp.where(sub == k, scale[k], scales)
        out.append(a[g] * scales)
    return jnp.concatenate(out, axis=0)[:, BLK:]


def left6(x):
    high, mid, low = split3(x)
    return jnp.concatenate([high, high, mid, mid, high, low], axis=1)


def right6(x, axis):
    high, mid, low = split3(x)
    return jnp.concatenate([high, mid, high, mid, low, high], axis=axis)


def factor_kernel(total_rows, core_ref, mine_ref, other_ref, w_ref, mean_ref, s_ref, spot_ref):
    core = core_ref[0]

    def assemble(halves):
        def get(tile):
            at = BLK * (tile % (TILES // 2))
            return halves[tile // (TILES // 2)][at : at + BLK, :] * (1.0 / total_rows)

        sums = get(TILES - 1)
        means = [sums[8 * j : 8 * j + 1, :] for j in range(FEAT // LANES)]
        turned = sums.T

        def mean_column(i):
            return turned[BLK * (i % 2) : BLK * (i % 2 + 1), 8 * (i // 2) : 8 * (i // 2) + 1]

        for tile, (i, j) in enumerate(WHOLE):
            s_ref[BLK * i : BLK * (i + 1), LANES * j : LANES * (j + 1)] = (
                get(tile) - mean_column(i) * means[j]
            )
        for n, pair in enumerate(PAIRED):
            both = get(len(WHOLE) + n)
            for side, i in enumerate(pair):
                part = both[:, BLK * side : BLK * (side + 1)]
                s_ref[BLK * i : BLK * (i + 1), BLK * i : BLK * (i + 1)] = (
                    part - mean_column(i) * means[i // 2][:, :BLK]
                )
        parts = split3(jnp.concatenate(means, axis=1))
        mean_ref[...] = jnp.concatenate(
            [p.astype(F32) for p in parts] + [jnp.zeros((13, FEAT), F32)], axis=0
        ).astype(BF16)

    @pl.when(core == 0)
    def _():
        assemble((mine_ref, other_ref))

    @pl.when(core == 1)
    def _():
        assemble((other_ref, mine_ref))

    w_ref[...] = jnp.zeros((FEAT, FEAT), F32)

    def trailing(k, inv6):
        at, to = BLK * k, BLK * (k + 1)
        below = nt(left6(s_ref[to:, at:to]), inv6)
        left, right = left6(below), right6(below, 1)
        for begin in range(0, FEAT - to, 256):
            end = min(begin + 256, FEAT - to)
            skip = BLK if begin == 0 else begin
            if skip < end:
                s_ref[to + skip : to + end, to : to + end] = s_ref[
                    to + skip : to + end, to : to + end
                ] - nt(left[skip:end], right[:end])
        w_ref[to:, :to] = w_ref[to:, :to] - nn(left, right6(w_ref[at:to, :to], 0))

    waiting = None
    for k in range(NBLK):
        at, to = BLK * k, BLK * (k + 1)
        inv = inverse_factor(s_ref[at:to, at:to], spot_ref)
        if waiting is not None:
            trailing(*waiting)
        inv6 = right6(inv, 1)
        if to < FEAT:
            first = nt(left6(s_ref[to : to + BLK, at:to]), inv6)
            s_ref[to : to + BLK, to : to + BLK] = s_ref[to : to + BLK, to : to + BLK] - nt(
                left6(first), right6(first, 1)
            )
            waiting = (k, inv6)
        if k:
            w_ref[at:to, :at] = nn(left6(inv), right6(w_ref[at:to, :at], 0))
        w_ref[at:to, at:to] = inv


def best_kernel(rows_ref, w_ref, mean_ref, best_ref, x_ref, z_ref, u_ref, sems):
    slots = rows_ref.shape[0]
    piece = slots // PIECES
    copies = [
        pltpu.make_async_copy(
            rows_ref.at[piece * i : piece * (i + 1)], x_ref.at[piece * i : piece * (i + 1)], sems.at[i]
        )
        for i in range(PIECES)
    ]
    for copy in copies:
        copy.start()
    parts = [split3(w_ref[256 * n : 256 * (n + 1), : 256 * (n + 1)]) for n in range(FEAT // 256)]

    def whiten(x, n):
        high, mid, low = parts[n]
        x = x[:, : 256 * (n + 1)]
        return nt(x, low) + nt(x, mid) + nt(x, high)

    shift = [
        jnp.sum(whiten(mean_ref[...], n), axis=0, keepdims=True) for n in range(FEAT // 256)
    ]
    for i, copy in enumerate(copies):
        copy.wait()
        here = slice(piece * i, piece * (i + 1))
        x = x_ref[here, :FEAT]
        norm = jnp.zeros((piece, 1), F32)
        for n in range(FEAT // 256):
            z = whiten(x, n) - shift[n]
            norm = norm + jnp.sum(z * z, axis=1, keepdims=True)
            z_ref[here, 256 * n : 256 * (n + 1)] = z
        u_ref[here, :] = (z_ref[here, :] * lax.rsqrt(norm + 1e-06)).astype(BF16)

    digits = x_ref[:, FEAT:]
    lane = lax.broadcasted_iota(jnp.int32, (2 * LANES, LANES), 1)
    upper = lax.broadcasted_iota(jnp.int32, (2 * LANES, LANES), 0) >= LANES
    low_weight = jnp.where(lane == 0, 1.0, jnp.where(lane == 1, 128.0, 0.0))
    high_weight = jnp.where(
        lane == 2, 1.0, jnp.where(lane == 3, 128.0, jnp.where(lane == 4, -16384.0, 0.0))
    )
    weight = jnp.where(upper, high_weight, low_weight).astype(BF16)
    down = nt(digits, weight).astype(jnp.int32)
    kkey = down[:, :LANES] + ((down[:, LANES:] + 16384) << 14)
    across = nt(weight, digits).astype(jnp.int32)
    qkey = across[0:1] + ((across[LANES : LANES + 1] + 16384) << 14)
    floor = qkey & ~(INDEX_SPAN - 1)
    best = jnp.full((1, slots), -1.0, F32)
    rows = 256
    for b in range(slots // rows):
        scores = nt(u_ref[rows * b : rows * (b + 1), :], u_ref[...])
        keys = kkey[rows * b : rows * (b + 1), :]
        found = []
        for c in range(0, slots, LANES):
            to = c + LANES
            allowed = (keys < qkey[:, c:to]) & (keys >= floor[:, c:to])
            found.append(
                jnp.max(jnp.where(allowed, scores[:, c:to], -1.0), axis=0, keepdims=True)
            )
        best = jnp.maximum(best, jnp.concatenate(found, axis=1))
    for o in range(slots // CAP):
        best_ref[o : o + 1, :] = best[:, CAP * o : CAP * (o + 1)]


def factor(core, mine, other, total_rows):
    return pl.pallas_call(
        functools.partial(factor_kernel, total_rows),
        out_shape=(
            jax.ShapeDtypeStruct((FEAT, FEAT), F32),
            jax.ShapeDtypeStruct((16, FEAT), BF16),
        ),
        in_specs=[SM, VM, VM],
        out_specs=(VM, VM),
        scratch_shapes=[pltpu.VMEM((FEAT, FEAT), F32), pltpu.VMEM((128, LANES), F32)],
        compiler_params=PARAMS,
        name="factor",
    )(core, mine, other)


def best_of(rows, inverse, mean):
    slots = rows.shape[0]
    return pl.pallas_call(
        best_kernel,
        out_shape=jax.ShapeDtypeStruct((slots // CAP, CAP), F32),
        in_specs=[ANY, VM, VM],
        out_specs=VM,
        scratch_shapes=[
            pltpu.VMEM((slots, WIDE), BF16),
            pltpu.VMEM((slots, FEAT), F32),
            pltpu.VMEM((slots, FEAT), BF16),
            pltpu.SemaphoreType.DMA((PIECES,)),
        ],
        compiler_params=PARAMS,
        name="best",
    )(rows, inverse, mean)


def unpack_kernel(best_ref, slot_ref, out_ref):
    best = best_ref[...]
    owners = best.shape[0]
    count = slot_ref.shape[1]
    slot = slot_ref[...]
    rank = jnp.broadcast_to(slot % CAP, (CAP, count))
    pick = jnp.where(lax.broadcasted_iota(jnp.int32, (CAP, count), 0) == rank, 1.0, 0.0)
    table = nn(best, pick.astype(F32), HIGHEST)
    owner = jnp.broadcast_to(slot // CAP, (owners, count))
    mine = lax.broadcasted_iota(jnp.int32, (owners, count), 0) == owner
    out_ref[...] = jnp.sum(jnp.where(mine, table, 0.0), axis=0, keepdims=True)


def unpack(best, slot):
    return pl.pallas_call(
        unpack_kernel,
        out_shape=jax.ShapeDtypeStruct(slot.shape, F32),
        in_specs=[VM, VM],
        out_specs=VM,
        compiler_params=PARAMS,
        name="unpack",
    )(best, slot)


def exchange(x, axis):
    return lax.all_to_all(x, axis, split_axis=0, concat_axis=0, tiled=True)


def on_device(embeddings, cluster_id, row_index):
    count = embeddings.shape[0]
    across, deep, highs = lax.axis_size("x"), lax.axis_size("z"), lax.axis_size("y")
    owners = 2 * highs
    total_rows = count * owners * across * deep
    shard, plane = ("y", "core"), ("x", "y")
    swap = [(0, 1), (1, 0)]
    core = lax.axis_index("core").astype(jnp.int32).reshape(1)
    keep, send = moments(core, embeddings)
    pair = keep + lax.ppermute(send, "core", swap)
    shares = across * highs
    share = HALF // shares
    pair, embeddings = lax.optimization_barrier((pair, embeddings))
    spread = exchange(pair.reshape(shares, share, LANES), plane)
    packed, slot = pack(embeddings, cluster_id, row_index, owners)
    part = jnp.sum(spread, axis=0)
    part, packed = lax.optimization_barrier((part, packed))
    column = exchange(jnp.broadcast_to(part[None], (deep, share, LANES)), "z")
    total = jnp.sum(column, axis=0)
    mine = exchange(jnp.broadcast_to(total[None], (shares, share, LANES)), plane)
    mine = mine.reshape(HALF, LANES)
    rows = exchange(packed.reshape(owners, CAP, WIDE), shard).reshape(owners * CAP, WIDE)
    other = lax.ppermute(mine, "core", swap)
    inverse, mean = factor(core, mine, other, total_rows)
    best = best_of(rows, inverse, mean)
    returned = exchange(best, shard)
    return unpack(returned, slot).reshape(count)


def solution(mesh):
    groups, shards = mesh.devices.shape
    deep = min(16, groups)
    split = Mesh(
        mesh.devices.reshape(groups // deep, deep, shards // 2, 2), ("x", "z", "y", "core")
    )
    rows = ("x", "z", "y", "core")
    return jax.shard_map(
        on_device,
        mesh=split,
        in_specs=(P(rows, None), P(rows), P(rows)),
        out_specs=P(rows),
        check_vma=False,
    )
```

profile of v0, /device:TPU:1, one launch (start us, length us, event | category | flops | bytes accessed | tf_op | source)
XLA Modules:
  0.0 167.0 jit_solution(11681497969215983642)
XLA Ops:
  0.0 0.0 copy-start
  0.0 1.1 copy-done
  1.1 1.2 moments.1
  2.3 0.0 copy-start.1
  2.3 0.0 copy-start.5
  2.3 0.0 copy-start.6
  2.3 16.2 %collective-permute-start = (f32[1280,128]{1,0:T(8,128)S(1)}, f32[1280,128]{1,0:T(8,128)S(1)}, u32[]{:S(2)}, u32[]{:S(2)}) collective-permute-start(f32[1280,128]{1,0:T(8,128)S(1)} %get-tuple-element.16), channel_id=1, source_target_pairs={{0,1},{1,0},{2,3},{3,2},{4,5},{5,4},{6,7},{7,6},{8,9},{9,8},{10,11... | collective-permute-start | bytes 1966088 | tf_op jit(solution)/shard_map/ppermute | solution.py:426
  18.5 1.7 %collective-permute-done = f32[1280,128]{1,0:T(8,128)S(1)} collective-permute-done((f32[1280,128]{1,0:T(8,128)S(1)}, f32[1280,128]{1,0:T(8,128)S(1)}, u32[]{:S(2)}, u32[]{:S(2)}) %collective-permute-start) | collective-permute-done | bytes 655392 | tf_op jit(solution)/shard_map/ppermute | solution.py:426
  20.2 0.9 add.3
  21.2 3.9 %all-to-all-start = ((f32[32,40,128]{2,1,0:T(8,128)}), f32[32,40,128]{2,1,0:T(8,128)S(1)}, u32[]{:S(2)}, u32[]{:S(2)}) async-start(f32[32,40,128]{2,1,0:T(8,128)} %bitcast.1), calls=%async_computation | async-start | bytes 1310720 | tf_op jit(solution)/shard_map/all_to_all | solution.py:414
  25.1 0.0 copy-done.1
  25.1 0.0 copy-done.5
  25.1 0.0 copy-done.6
  25.1 1.4 pack_rows.1
  26.5 0.0 copy-start.4
  26.5 1.2 copy-done.4
  27.8 14.2 %all-to-all-done = f32[32,40,128]{2,1,0:T(8,128)S(1)} async-done(((f32[32,40,128]{2,1,0:T(8,128)}), f32[32,40,128]{2,1,0:T(8,128)S(1)}, u32[]{:S(2)}, u32[]{:S(2)}) %all-to-all-start) | async-done | bytes 655392 | tf_op jit(solution)/shard_map/all_to_all | solution.py:414
  42.0 0.1 reduce_sum.18
  42.1 25.0 %all_to_all.31 = f32[16,40,128]{2,1,0:T(8,128)S(1)} all-to-all(f32[16,40,128]{2,1,0:T(8,128)S(1)} %broadcast_in_dim.4), channel_id=1, replica_groups=mesh['x'=4,'z'=16,'y'=8,'core'=2] {'z'}, dimensions={0} | all-to-all | bytes 655360 | tf_op jit(solution)/shard_map/all_to_all | solution.py:414
  67.1 23.0 %all_to_all.32 = f32[32,40,128]{2,1,0:T(8,128)S(1)} all-to-all(f32[32,40,128]{2,1,0:T(8,128)S(1)} %broadcast_in_dim.5), channel_id=1, replica_groups=mesh['x'=4,'z'=16,'y'=8,'core'=2] {'x','y'}, dimensions={0} | all-to-all | bytes 1310720 | tf_op jit(solution)/shard_map/all_to_all | solution.py:414
  90.1 12.2 %all-to-all-start.1 = ((bf16[16,64,896]{2,1,0:T(8,128)(2,1)}), bf16[16,64,896]{2,1,0:T(8,128)(2,1)S(1)}, u32[]{:S(2)}, u32[]{:S(2)}) async-start(bf16[16,64,896]{2,1,0:T(8,128)(2,1)} %bitcast.15), calls=%async_computation.1 | async-start | bytes 3670016 | tf_op jit(solution)/shard_map/all_to_all | solution.py:414
  102.3 2.1 %collective-permute-start.1 = (f32[1280,128]{1,0:T(8,128)S(1)}, f32[1280,128]{1,0:T(8,128)S(1)}, u32[]{:S(2)}, u32[]{:S(2)}) collective-permute-start(f32[1280,128]{1,0:T(8,128)S(1)} %bitcast.13), channel_id=1, source_target_pairs={{0,1},{1,0},{2,3},{3,2},{4,5},{5,4},{6,7},{7,6},{8,9},{9,8},{10,11... | collective-permute-start | bytes 1966088 | tf_op jit(solution)/shard_map/ppermute | solution.py:439
  104.4 1.8 %collective-permute-done.1.other_ref = f32[1280,128]{1,0:T(8,128)S(1)} collective-permute-done((f32[1280,128]{1,0:T(8,128)S(1)}, f32[1280,128]{1,0:T(8,128)S(1)}, u32[]{:S(2)}, u32[]{:S(2)}) %collective-permute-start.1) | collective-permute-done | bytes 655392 | tf_op jit(solution)/shard_map/ppermute | solution.py:439
  106.3 25.7 %factor.1 = (f32[768,768]{1,0:T(8,128)S(1)}, bf16[16,768]{1,0:T(8,128)(2,1)S(1)}) custom-call(s32[1]{0:T(128)} %bitcast.core_ref, f32[1280,128]{1,0:T(8,128)S(1)} %bitcast.14, f32[1280,128]{1,0:T(8,128)S(1)} %collective-permute-done.1.other_ref), custom_call_target="tpu_custom_call" | custom-call | tf_op jit(solution)/shard_map/factor/pallas_call | solution.py:357
  132.0 0.0 copy-start.2
  132.0 1.4 copy-done.2
  133.4 12.6 %all-to-all-done.1 = bf16[16,64,896]{2,1,0:T(8,128)(2,1)S(1)} async-done(((bf16[16,64,896]{2,1,0:T(8,128)(2,1)}), bf16[16,64,896]{2,1,0:T(8,128)(2,1)S(1)}, u32[]{:S(2)}, u32[]{:S(2)}) %all-to-all-start.1) | async-done | bytes 1835040 | tf_op jit(solution)/shard_map/all_to_all | solution.py:414
  146.0 0.0 copy-start.3
  146.0 1.7 copy-done.3
  147.7 7.0 %best.1 = f32[16,64]{1,0:T(8,128)S(1)} custom-call(bf16[1024,896]{1,0:T(8,128)(2,1)S(1)} %bitcast.12, f32[768,768]{1,0:T(8,128)S(1)} %copy-done.3, bf16[16,768]{1,0:T(8,128)(2,1)S(1)} %get-tuple-element.23.mean_ref), custom_call_target="tpu_custom_call" | custom-call | tf_op jit(solution)/shard_map/best/pallas_call | solution.py:373
  154.7 11.5 %all_to_all.33 = f32[16,1,64]{2,1,0:T(1,128)S(1)} all-to-all(f32[16,1,64]{2,1,0:T(1,128)S(1)} %bitcast.16), channel_id=1, replica_groups=mesh['x'=4,'z'=16,'y'=8,'core'=2] {'y','core'}, dimensions={0} | all-to-all | bytes 8192 | tf_op jit(solution)/shard_map/all_to_all | solution.py:414
  166.2 0.8 unpack.1
  (3 shorter events, 0.1 us)
Async XLA Ops:
  0.0 1.1 copy-start
  2.3 22.8 %copy-start.1 = (bf16[512,768]{1,0:T(8,128)(2,1)S(1)}, bf16[512,768]{1,0:T(8,128)(2,1)}, u32[]{:S(2)}) copy-start(bf16[512,768]{1,0:T(8,128)(2,1)} %x_ref.2) | copy-start | bytes 2359300
  2.3 22.8 %copy-start.5 = (s32[512]{0:T(512)S(1)}, s32[512]{0:T(512)}, u32[]{:S(2)}) copy-start(s32[512]{0:T(512)} %param.4) | copy-start | bytes 6148
  2.3 22.8 %copy-start.6 = (s32[512]{0:T(512)S(1)}, s32[512]{0:T(512)}, u32[]{:S(2)}) copy-start(s32[512]{0:T(512)} %param.5) | copy-start | bytes 6148
  2.3 17.9 %collective-permute-start = (f32[1280,128]{1,0:T(8,128)S(1)}, f32[1280,128]{1,0:T(8,128)S(1)}, u32[]{:S(2)}, u32[]{:S(2)}) collective-permute-start(f32[1280,128]{1,0:T(8,128)S(1)} %get-tuple-element.16), channel_id=1, source_target_pairs={{0,1},{1,0},{2,3},{3,2},{4,5},{5,4},{6,7},{7,6},{8,9},{9,8},{10,11... | collective-permute-start | bytes 1966088 | tf_op jit(solution)/shard_map/ppermute | solution.py:426
  21.2 20.8 %all-to-all-start = ((f32[32,40,128]{2,1,0:T(8,128)}), f32[32,40,128]{2,1,0:T(8,128)S(1)}, u32[]{:S(2)}, u32[]{:S(2)}) async-start(f32[32,40,128]{2,1,0:T(8,128)} %bitcast.1), calls=%async_computation | async-start | bytes 1310720 | tf_op jit(solution)/shard_map/all_to_all | solution.py:414
  26.5 1.2 copy-start.4
  90.1 55.9 %all-to-all-start.1 = ((bf16[16,64,896]{2,1,0:T(8,128)(2,1)}), bf16[16,64,896]{2,1,0:T(8,128)(2,1)S(1)}, u32[]{:S(2)}, u32[]{:S(2)}) async-start(bf16[16,64,896]{2,1,0:T(8,128)(2,1)} %bitcast.15), calls=%async_computation.1 | async-start | bytes 3670016 | tf_op jit(solution)/shard_map/all_to_all | solution.py:414
  102.3 4.0 %collective-permute-start.1 = (f32[1280,128]{1,0:T(8,128)S(1)}, f32[1280,128]{1,0:T(8,128)S(1)}, u32[]{:S(2)}, u32[]{:S(2)}) collective-permute-start(f32[1280,128]{1,0:T(8,128)S(1)} %bitcast.13), channel_id=1, source_target_pairs={{0,1},{1,0},{2,3},{3,2},{4,5},{5,4},{6,7},{7,6},{8,9},{9,8},{10,11... | collective-permute-start | bytes 1966088 | tf_op jit(solution)/shard_map/ppermute | solution.py:439
  132.0 1.4 copy-start.2
  146.0 1.7 copy-start.3
where the time goes:
time: 170 us; the launch traced here: 167 us
  blocking collectives  59.4 us (35%)
  Pallas kernels  36.1 us (21%)
  starting transfers between devices  34.4 us (20%)
  waiting for transfers between devices  30.4 us (18%)
  local copies, waits for them, and re-layouts  5.52 us (3%)
    all_to_all x3, blocking collectives, exchange(): return lax.all_to_all(x, axis, split_axis=0, concat_axis=0, tiled=True)  59.4 us
    all_to_all x2, waiting for transfers between devices, exchange(): return lax.all_to_all(x, axis, split_axis=0, concat_axis=0, tiled=True)  26.8 us
    pallas_call x1, Pallas kernels, factor(): pl.pallas_call(functools.partial(factor_kernel, total_rows), out_shape=(j...  25.7 us
    ppermute x1, starting transfers between devices, on_device(): pair = keep + lax.ppermute(send, 'core', swap)  16.2 us
    all_to_all x2, starting transfers between devices, exchange(): return lax.all_to_all(x, axis, split_axis=0, concat_axis=0, tiled=True)  16.1 us
    pallas_call x1, Pallas kernels, best_of(): pl.pallas_call(best_kernel, out_shape=jax.ShapeDtypeStruct((slots // CAP,...  7.04 us
    unnamed x14, local copies, waits for them, and re-layouts  5.45 us
  transfers between devices with their start and end apart: 4, of which 4 were waited for; matrix products, arithmetic and copies ran while one was open for 0% of the time, Pallas kernels for 16%

commit v1 on v0

--- a/solution.py
+++ b/solution.py
@@ -18,15 +18,18 @@
 PAIRED = [(i, i + 2) for i in range(0, NBLK, 4)]
 TILES = len(WHOLE) + len(PAIRED) + 1
 HALF = TILES // 2 * BLK
+QUARTER = HALF // 4
 WIDE = FEAT + LANES
 CAP = 64
 CL_OWN = 8
 INDEX_SPAN = 2**19
 PIECES = 2
+DEEP = 16
 HIGHEST = lax.Precision.HIGHEST
 VM = pl.BlockSpec(memory_space=pltpu.VMEM)
 SM = pl.BlockSpec(memory_space=pltpu.SMEM)
 ANY = pl.BlockSpec(memory_space=pl.ANY)
+HBM = pl.BlockSpec(memory_space=pltpu.HBM)
 PARAMS = pltpu.CompilerParams(vmem_limit_bytes=24 * 2**20)
 
 
@@ -174,15 +177,13 @@
         for k in range(0, 8, 2):
             p, q, t = s[k, k], s[k, k + 1], s[k + 1, k + 1]
             det = p * t - q * q
-            guess = pl.reciprocal(det, approx=True)
-            fix = 2.0 - det * guess
-            over = guess * fix
+            over = pl.reciprocal(det, approx=True)
             ua = {l: s[k, l] * t - s[k + 1, l] * q for l in range(k + 2, 8)}
             ub = {l: s[k + 1, l] * p - s[k, l] * q for l in range(k + 2, 8)}
             for l in range(k + 2, 8):
                 for n in range(l, 8):
                     num = ua[l] * s[k, n] + ub[l] * s[k + 1, n]
-                    s[l, n] = s[l, n] - (num * guess) * fix
+                    s[l, n] = s[l, n] - num * over
             root = lax.rsqrt(p)
             scale[k] = root
             scale[k + 1] = lax.rsqrt(det) * (p * root)
@@ -219,44 +220,55 @@
     return jnp.concatenate([high, mid, high, mid, low, high], axis=axis)
 
 
-def factor_kernel(total_rows, core_ref, mine_ref, other_ref, w_ref, mean_ref, s_ref, spot_ref):
-    core = core_ref[0]
-
-    def assemble(halves):
-        def get(tile):
-            at = BLK * (tile % (TILES // 2))
-            return halves[tile // (TILES // 2)][at : at + BLK, :] * (1.0 / total_rows)
-
-        sums = get(TILES - 1)
-        means = [sums[8 * j : 8 * j + 1, :] for j in range(FEAT // LANES)]
-        turned = sums.T
-
-        def mean_column(i):
-            return turned[BLK * (i % 2) : BLK * (i % 2 + 1), 8 * (i // 2) : 8 * (i // 2) + 1]
-
-        for tile, (i, j) in enumerate(WHOLE):
-            s_ref[BLK * i : BLK * (i + 1), LANES * j : LANES * (j + 1)] = (
-                get(tile) - mean_column(i) * means[j]
+def factor_kernel(
+    total_rows, place_ref, near_ref, far_ref, near2_ref, far2_ref, out_ref, mean_ref, tri_ref, s_ref, w_ref, spot_ref, sems
+):
+    core, column = place_ref[0], place_ref[1]
+    copies = []
+    for side, parts in ((core, (near_ref, far_ref)), (1 - core, (near2_ref, far2_ref))):
+        spot = 0
+        for part in parts:
+            for at in range(0, part.shape[0], QUARTER):
+                piece = column ^ (spot ^ (spot >> 1))
+                copies.append(
+                    pltpu.make_async_copy(
+                        part.at[at : at + QUARTER],
+                        tri_ref.at[side, pl.ds(pl.multiple_of(piece * QUARTER, QUARTER), QUARTER)],
+                        sems.at[len(copies)],
+                    )
+                )
+                spot += 1
+    for copy in copies:
+        copy.start()
+    for copy in copies:
+        copy.wait()
+
+    def get(tile):
+        at = BLK * (tile % (TILES // 2))
+        return tri_ref[tile // (TILES // 2), at : at + BLK, :] * (1.0 / total_rows)
+
+    sums = get(TILES - 1)
+    means = [sums[8 * j : 8 * j + 1, :] for j in range(FEAT // LANES)]
+    turned = sums.T
+
+    def mean_column(i):
+        return turned[BLK * (i % 2) : BLK * (i % 2 + 1), 8 * (i // 2) : 8 * (i // 2) + 1]
+
+    for tile, (i, j) in enumerate(WHOLE):
+        s_ref[BLK * i : BLK * (i + 1), LANES * j : LANES * (j + 1)] = (
+            get(tile) - mean_column(i) * means[j]
+        )
+    for n, pair in enumerate(PAIRED):
+        both = get(len(WHOLE) + n)
+        for side, i in enumerate(pair):
+            part = both[:, BLK * side : BLK * (side + 1)]
+            s_ref[BLK * i : BLK * (i + 1), BLK * i : BLK * (i + 1)] = (
+                part - mean_column(i) * means[i // 2][:, :BLK]
             )
-        for n, pair in enumerate(PAIRED):
-            both = get(len(WHOLE) + n)
-            for side, i in enumerate(pair):
-                part = both[:, BLK * side : BLK * (side + 1)]
-                s_ref[BLK * i : BLK * (i + 1), BLK * i : BLK * (i + 1)] = (
-                    part - mean_column(i) * means[i // 2][:, :BLK]
-                )
-        parts = split3(jnp.concatenate(means, axis=1))
-        mean_ref[...] = jnp.concatenate(
-            [p.astype(F32) for p in parts] + [jnp.zeros((13, FEAT), F32)], axis=0
-        ).astype(BF16)
-
-    @pl.when(core == 0)
-    def _():
-        assemble((mine_ref, other_ref))
-
-    @pl.when(core == 1)
-    def _():
-        assemble((other_ref, mine_ref))
+    parts = split3(jnp.concatenate(means, axis=1))
+    mean_ref[...] = jnp.concatenate(
+        [p.astype(F32) for p in parts] + [jnp.zeros((13, FEAT), F32)], axis=0
+    ).astype(BF16)
 
     w_ref[...] = jnp.zeros((FEAT, FEAT), F32)
 
@@ -274,6 +286,7 @@
         w_ref[to:, :to] = w_ref[to:, :to] - nn(left, right6(w_ref[at:to, :to], 0))
 
     waiting = None
+    leaving = []
     for k in range(NBLK):
         at, to = BLK * k, BLK * (k + 1)
         inv = inverse_factor(s_ref[at:to, at:to], spot_ref)
@@ -289,9 +302,17 @@
         if k:
             w_ref[at:to, :at] = nn(left6(inv), right6(w_ref[at:to, :at], 0))
         w_ref[at:to, at:to] = inv
-
-
-def best_kernel(rows_ref, w_ref, mean_ref, best_ref, x_ref, z_ref, u_ref, sems):
+        if to % 256 == 0:
+            copy = pltpu.make_async_copy(
+                w_ref.at[to - 256 : to, 0:to], out_ref.at[to - 256 : to, 0:to], sems.at[to // 256 - 1]
+            )
+            copy.start()
+            leaving.append(copy)
+    for copy in leaving:
+        copy.wait()
+
+
+def best_kernel(rows_ref, inverse_ref, mean_ref, best_ref, w_ref, x_ref, z_ref, u_ref, sems):
     slots = rows_ref.shape[0]
     piece = slots // PIECES
     copies = [
@@ -300,9 +321,20 @@
         )
         for i in range(PIECES)
     ]
-    for copy in copies:
+    fetch = [
+        pltpu.make_async_copy(
+            inverse_ref.at[256 * n : 256 * (n + 1), 0 : 256 * (n + 1)],
+            w_ref.at[256 * n : 256 * (n + 1), 0 : 256 * (n + 1)],
+            sems.at[PIECES + n],
+        )
+        for n in range(FEAT // 256)
+    ]
+    for copy in fetch + copies:
         copy.start()
-    parts = [split3(w_ref[256 * n : 256 * (n + 1), : 256 * (n + 1)]) for n in range(FEAT // 256)]
+    parts = []
+    for n in range(FEAT // 256):
+        fetch[n].wait()
+        parts.append(split3(w_ref[256 * n : 256 * (n + 1), : 256 * (n + 1)]))
 
     def whiten(x, n):
         high, mid, low = parts[n]
@@ -353,19 +385,25 @@
         best_ref[o : o + 1, :] = best[:, CAP * o : CAP * (o + 1)]
 
 
-def factor(core, mine, other, total_rows):
+def factor(place, pieces, total_rows):
     return pl.pallas_call(
         functools.partial(factor_kernel, total_rows),
         out_shape=(
             jax.ShapeDtypeStruct((FEAT, FEAT), F32),
             jax.ShapeDtypeStruct((16, FEAT), BF16),
         ),
-        in_specs=[SM, VM, VM],
-        out_specs=(VM, VM),
-        scratch_shapes=[pltpu.VMEM((FEAT, FEAT), F32), pltpu.VMEM((128, LANES), F32)],
+        in_specs=[SM, ANY, ANY, ANY, ANY],
+        out_specs=(HBM, VM),
+        scratch_shapes=[
+            pltpu.VMEM((2, HALF, LANES), F32),
+            pltpu.VMEM((FEAT, FEAT), F32),
+            pltpu.VMEM((FEAT, FEAT), F32),
+            pltpu.VMEM((128, LANES), F32),
+            pltpu.SemaphoreType.DMA((8,)),
+        ],
         compiler_params=PARAMS,
         name="factor",
-    )(core, mine, other)
+    )(place, *pieces)
 
 
 def best_of(rows, inverse, mean):
@@ -373,13 +411,14 @@
     return pl.pallas_call(
         best_kernel,
         out_shape=jax.ShapeDtypeStruct((slots // CAP, CAP), F32),
-        in_specs=[ANY, VM, VM],
+        in_specs=[HBM, HBM, VM],
         out_specs=VM,
         scratch_shapes=[
+            pltpu.VMEM((FEAT, FEAT), F32),
             pltpu.VMEM((slots, WIDE), BF16),
             pltpu.VMEM((slots, FEAT), F32),
             pltpu.VMEM((slots, FEAT), BF16),
-            pltpu.SemaphoreType.DMA((PIECES,)),
+            pltpu.SemaphoreType.DMA((PIECES + FEAT // 256,)),
         ],
         compiler_params=PARAMS,
         name="best",
@@ -421,8 +460,9 @@
     total_rows = count * owners * across * deep
     shard, plane = ("y", "core"), ("x", "y")
     swap = [(0, 1), (1, 0)]
-    core = lax.axis_index("core").astype(jnp.int32).reshape(1)
-    keep, send = moments(core, embeddings)
+    core = lax.axis_index("core").astype(jnp.int32)
+    column = lax.axis_index("x").astype(jnp.int32)
+    keep, send = moments(core.reshape(1), embeddings)
     pair = keep + lax.ppermute(send, "core", swap)
     shares = across * highs
     share = HALF // shares
@@ -431,13 +471,17 @@
     packed, slot = pack(embeddings, cluster_id, row_index, owners)
     part = jnp.sum(spread, axis=0)
     part, packed = lax.optimization_barrier((part, packed))
-    column = exchange(jnp.broadcast_to(part[None], (deep, share, LANES)), "z")
-    total = jnp.sum(column, axis=0)
-    mine = exchange(jnp.broadcast_to(total[None], (shares, share, LANES)), plane)
-    mine = mine.reshape(HALF, LANES)
+    total = jnp.sum(exchange(jnp.broadcast_to(part[None], (deep, share, LANES)), "z"), axis=0)
+    quarter = exchange(jnp.broadcast_to(total[None], (highs, share, LANES)), "y")
+    quarter = quarter.reshape(highs * share, LANES)
     rows = exchange(packed.reshape(owners, CAP, WIDE), shard).reshape(owners * CAP, WIDE)
-    other = lax.ppermute(mine, "core", swap)
-    inverse, mean = factor(core, mine, other, total_rows)
+    beside = lax.ppermute(quarter, "x", [(i, i ^ 1) for i in range(across)])
+    near = jnp.concatenate([quarter, beside], axis=0)
+    far = lax.ppermute(near, "x", [(i, i ^ 3) for i in range(across)])
+    near2 = lax.ppermute(near, "core", swap)
+    far2 = lax.ppermute(far, "core", swap)
+    place = jnp.stack([core, column])
+    inverse, mean = factor(place, (near, far, near2, far2), total_rows)
     best = best_of(rows, inverse, mean)
     returned = exchange(best, shard)
     return unpack(returned, slot).reshape(count)
@@ -445,7 +489,7 @@
 
 def solution(mesh):
     groups, shards = mesh.devices.shape
-    deep = min(16, groups)
+    deep = min(DEEP, groups)
     split = Mesh(
         mesh.devices.reshape(groups // deep, deep, shards // 2, 2), ("x", "z", "y", "core")
     )

time: 170 us -> 171 us (level); the launches traced: 167 us -> 170 us
  starting transfers between devices: 34.4 us -> 44.4 us
  blocking collectives: 59.4 us -> 54.9 us
  waiting for transfers between devices: 30.4 us -> 26.8 us
    all_to_all x2, waiting for transfers between devices: 26.8 us -> 14.2 us  [exchange(): return lax.all_to_all(x, axis, split_axis=0, concat_axis=0, tiled=True)]
    ppermute x1 -> x4, starting transfers between devices: 2.13 us -> 12.9 us  [the longest x1 3.87 us: on_device(): far2 = lax.ppermute(far, 'core', swap)]
    ppermute x1 -> x4, waiting for transfers between devices: 1.84 us -> 10.8 us  [the longest x1 5.14 us: on_device(): beside = lax.ppermute(quarter, 'x', [(i, i ^ 1) for i in range(across)])]
    all_to_all x3, blocking collectives: 59.4 us -> 54.9 us  [exchange(): return lax.all_to_all(x, axis, split_axis=0, concat_axis=0, tiled=True)]
  transfers between devices with their start and end apart: 4 -> 7, of which waited for: 4 -> 5; matrix products, arithmetic and copies ran while one was open for 0% -> 0% of each run, Pallas kernels for 16% -> 16%
where the time goes in v1:
time: 171 us; the launch traced here: 170 us
  blocking collectives  54.9 us (32%)
  starting transfers between devices  44.4 us (26%)
  Pallas kernels  37.1 us (22%)
  waiting for transfers between devices  26.8 us (16%)
  local copies, waits for them, and re-layouts  5.49 us (3%)
    all_to_all x3, blocking collectives, exchange(): return lax.all_to_all(x, axis, split_axis=0, concat_axis=0, tiled=True)  54.9 us
    pallas_call x1, Pallas kernels, factor(): pl.pallas_call(functools.partial(factor_kernel, total_rows), out_shape=(j...  26.1 us
    ppermute x1, starting transfers between devices, on_device(): pair = keep + lax.ppermute(send, 'core', swap)  16.2 us
    all_to_all x2, starting transfers between devices, exchange(): return lax.all_to_all(x, axis, split_axis=0, concat_axis=0, tiled=True)  15.3 us
    all_to_all x2, waiting for transfers between devices, exchange(): return lax.all_to_all(x, axis, split_axis=0, concat_axis=0, tiled=True)  14.2 us
    pallas_call x1, Pallas kernels, best_of(): pl.pallas_call(best_kernel, out_shape=jax.ShapeDtypeStruct((slots // CAP,...  7.62 us
    unnamed x14, local copies, waits for them, and re-layouts  5.45 us
    ppermute x1, waiting for transfers between devices, on_device(): beside = lax.ppermute(quarter, 'x', [(i, i ^ 1) for i in range(across)])  5.14 us
  transfers between devices with their start and end apart: 7, of which 5 were waited for; matrix products, arithmetic and copies ran while one was open for 0% of the time, Pallas kernels for 16%

profile of v1, /device:TPU:1, one launch (start us, length us, event | category | flops | bytes accessed | tf_op | source)
XLA Modules:
  0.0 170.0 jit_solution(10759774276505367817)
XLA Ops:
  0.0 0.0 copy-start
  0.0 1.1 copy-done
  1.1 1.2 moments.1
  2.3 0.0 copy-start.1
  2.3 0.0 copy-start.5
  2.3 0.0 copy-start.6
  2.3 16.2 %collective-permute-start = (f32[1280,128]{1,0:T(8,128)S(1)}, f32[1280,128]{1,0:T(8,128)S(1)}, u32[]{:S(2)}, u32[]{:S(2)}) collective-permute-start(f32[1280,128]{1,0:T(8,128)S(1)} %get-tuple-element.16), channel_id=1, source_target_pairs={{0,1},{1,0},{2,3},{3,2},{4,5},{5,4},{6,7},{7,6},{8,9},{9,8},{10,11... | collective-permute-start | bytes 1966088 | tf_op jit(solution)/shard_map/ppermute | solution.py:466
  18.5 1.7 %collective-permute-done = f32[1280,128]{1,0:T(8,128)S(1)} collective-permute-done((f32[1280,128]{1,0:T(8,128)S(1)}, f32[1280,128]{1,0:T(8,128)S(1)}, u32[]{:S(2)}, u32[]{:S(2)}) %collective-permute-start) | collective-permute-done | bytes 655392 | tf_op jit(solution)/shard_map/ppermute | solution.py:466
  20.2 0.9 add.3
  21.2 3.9 %all-to-all-start = ((f32[32,40,128]{2,1,0:T(8,128)}), f32[32,40,128]{2,1,0:T(8,128)S(1)}, u32[]{:S(2)}, u32[]{:S(2)}) async-start(f32[32,40,128]{2,1,0:T(8,128)} %bitcast.1), calls=%async_computation | async-start | bytes 1310720 | tf_op jit(solution)/shard_map/all_to_all | solution.py:453
  25.1 0.0 copy-done.1
  25.1 0.0 copy-done.5
  25.1 0.0 copy-done.6
  25.1 1.4 pack_rows.1
  26.5 0.0 copy-start.4
  26.5 1.2 copy-done.4
  27.8 14.2 %all-to-all-done = f32[32,40,128]{2,1,0:T(8,128)S(1)} async-done(((f32[32,40,128]{2,1,0:T(8,128)}), f32[32,40,128]{2,1,0:T(8,128)S(1)}, u32[]{:S(2)}, u32[]{:S(2)}) %all-to-all-start) | async-done | bytes 655392 | tf_op jit(solution)/shard_map/all_to_all | solution.py:453
  42.0 0.1 reduce_sum.18
  42.1 25.0 %all_to_all.31 = f32[16,40,128]{2,1,0:T(8,128)S(1)} all-to-all(f32[16,40,128]{2,1,0:T(8,128)S(1)} %broadcast_in_dim.4), channel_id=1, replica_groups=mesh['x'=4,'z'=16,'y'=8,'core'=2] {'z'}, dimensions={0} | all-to-all | bytes 655360 | tf_op jit(solution)/shard_map/all_to_all | solution.py:453
  67.1 16.0 %all_to_all.32 = f32[8,40,128]{2,1,0:T(8,128)S(1)} all-to-all(f32[8,40,128]{2,1,0:T(8,128)S(1)} %broadcast_in_dim.5), channel_id=1, replica_groups=mesh['x'=4,'z'=16,'y'=8,'core'=2] {'y'}, dimensions={0} | all-to-all | bytes 327680 | tf_op jit(solution)/shard_map/all_to_all | solution.py:453
  83.1 11.4 %all-to-all-start.1 = ((bf16[16,64,896]{2,1,0:T(8,128)(2,1)}), bf16[16,64,896]{2,1,0:T(8,128)(2,1)S(1)}, u32[]{:S(2)}, u32[]{:S(2)}) async-start(bf16[16,64,896]{2,1,0:T(8,128)(2,1)} %bitcast.14), calls=%async_computation.1 | async-start | bytes 3670016 | tf_op jit(solution)/shard_map/all_to_all | solution.py:453
  94.5 2.3 %collective-permute-start.1 = (f32[320,128]{1,0:T(8,128)S(1)}, f32[320,128]{1,0:T(8,128)S(1)}, u32[]{:S(2)}, u32[]{:S(2)}) collective-permute-start(f32[320,128]{1,0:T(8,128)S(1)} %bitcast.19), channel_id=1, source_target_pairs={{0,256},{256,0},{512,768},{768,512},{1,257},{257,1},{513,769},{769... | collective-permute-start | bytes 491528 | tf_op jit(solution)/shard_map/ppermute | solution.py:478
  96.8 5.1 %collective-permute-done.1 = f32[320,128]{1,0:T(8,128)S(1)} collective-permute-done((f32[320,128]{1,0:T(8,128)S(1)}, f32[320,128]{1,0:T(8,128)S(1)}, u32[]{:S(2)}, u32[]{:S(2)}) %collective-permute-start.1) | collective-permute-done | bytes 163872 | tf_op jit(solution)/shard_map/ppermute | solution.py:478
  102.0 3.5 %collective-permute-start.2 = (f32[640,128]{1,0:T(8,128)S(1)}, f32[640,128]{1,0:T(8,128)S(1)}, u32[]{:S(2)}, u32[]{:S(2)}) collective-permute-start(f32[640,128]{1,0:T(8,128)S(1)} %pad_maximum_fusion.near_ref), channel_id=1, source_target_pairs={{0,768},{256,512},{512,256},{768,0},{1,769},{257,513},{513,257},{7... | collective-permute-start | bytes 983048 | tf_op jit(solution)/shard_map/ppermute | solution.py:480
  105.5 3.2 %collective-permute-start.3 = (f32[640,128]{1,0:T(8,128)S(1)}, f32[640,128]{1,0:T(8,128)S(1)}, u32[]{:S(2)}, u32[]{:S(2)}) collective-permute-start(f32[640,128]{1,0:T(8,128)S(1)} %pad_maximum_fusion.near_ref), channel_id=1, source_target_pairs={{0,1},{1,0},{2,3},{3,2},{4,5},{5,4},{6,7},{7,6},{8,9},{9,8},{10,11... | collective-permute-start | bytes 983048 | tf_op jit(solution)/shard_map/ppermute | solution.py:481
  108.7 4.6 %collective-permute-done.2.far_ref = f32[640,128]{1,0:T(8,128)S(1)} collective-permute-done((f32[640,128]{1,0:T(8,128)S(1)}, f32[640,128]{1,0:T(8,128)S(1)}, u32[]{:S(2)}, u32[]{:S(2)}) %collective-permute-start.2) | collective-permute-done | bytes 327712 | tf_op jit(solution)/shard_map/ppermute | solution.py:480
  113.3 3.9 %collective-permute-start.4 = (f32[640,128]{1,0:T(8,128)S(1)}, f32[640,128]{1,0:T(8,128)S(1)}, u32[]{:S(2)}, u32[]{:S(2)}) collective-permute-start(f32[640,128]{1,0:T(8,128)S(1)} %collective-permute-done.2.far_ref), channel_id=1, source_target_pairs={{0,1},{1,0},{2,3},{3,2},{4,5},{5,4},{6,7},{7,6},{8,9},{9,8},{10,11... | collective-permute-start | bytes 983048 | tf_op jit(solution)/shard_map/ppermute | solution.py:482
  117.1 0.1 pad_add_fusion.place_ref
  117.2 0.0 collective-permute-done.3.near2_ref
  117.2 1.2 collective-permute-done.4.far2_ref
  118.4 26.1 %factor.1 = (f32[768,768]{1,0:T(8,128)S(1)}, bf16[16,768]{1,0:T(8,128)(2,1)S(1)}) custom-call(s32[2]{0:T(128)S(1)} %pad_add_fusion.place_ref, f32[640,128]{1,0:T(8,128)S(1)} %pad_maximum_fusion.near_ref, f32[640,128]{1,0:T(8,128)S(1)} %collective-permute-done.2.far_ref, f32[640,128]{1,0:T(8,128)S(1)} %collective-permute-done.3.near2_ref, ...), custom_call_target="tpu_custom_call" | custom-call | tf_op jit(solution)/shard_map/factor/pallas_call | solution.py:389
  144.5 0.0 copy-start.2
  144.5 1.4 copy-done.2
  145.9 0.0 all-to-all-done.1
  145.9 0.0 copy-start.3
  145.9 1.7 copy-done.3
  147.6 7.6 %best.1 = f32[16,64]{1,0:T(8,128)S(1)} custom-call(bf16[1024,896]{1,0:T(8,128)(2,1)S(1)} %bitcast.13, f32[768,768]{1,0:T(8,128)S(1)} %copy-done.3, bf16[16,768]{1,0:T(8,128)(2,1)S(1)} %get-tuple-element.23.mean_ref), custom_call_target="tpu_custom_call" | custom-call | tf_op jit(solution)/shard_map/best/pallas_call | solution.py:411
  155.2 13.9 %all_to_all.33 = f32[16,1,64]{2,1,0:T(1,128)S(1)} all-to-all(f32[16,1,64]{2,1,0:T(1,128)S(1)} %bitcast.15), channel_id=1, replica_groups=mesh['x'=4,'z'=16,'y'=8,'core'=2] {'y','core'}, dimensions={0} | all-to-all | bytes 8192 | tf_op jit(solution)/shard_map/all_to_all | solution.py:453
  169.2 0.8 unpack.1
  (4 shorter events, 0.1 us)
Async XLA Ops:
  0.0 1.1 copy-start
  2.3 22.8 %copy-start.1 = (bf16[512,768]{1,0:T(8,128)(2,1)S(1)}, bf16[512,768]{1,0:T(8,128)(2,1)}, u32[]{:S(2)}) copy-start(bf16[512,768]{1,0:T(8,128)(2,1)} %x_ref.2) | copy-start | bytes 2359300
  2.3 22.8 %copy-start.5 = (s32[512]{0:T(512)S(1)}, s32[512]{0:T(512)}, u32[]{:S(2)}) copy-start(s32[512]{0:T(512)} %param.4) | copy-start | bytes 6148
  2.3 22.8 %copy-start.6 = (s32[512]{0:T(512)S(1)}, s32[512]{0:T(512)}, u32[]{:S(2)}) copy-start(s32[512]{0:T(512)} %param.5) | copy-start | bytes 6148
  2.3 17.9 %collective-permute-start = (f32[1280,128]{1,0:T(8,128)S(1)}, f32[1280,128]{1,0:T(8,128)S(1)}, u32[]{:S(2)}, u32[]{:S(2)}) collective-permute-start(f32[1280,128]{1,0:T(8,128)S(1)} %get-tuple-element.16), channel_id=1, source_target_pairs={{0,1},{1,0},{2,3},{3,2},{4,5},{5,4},{6,7},{7,6},{8,9},{9,8},{10,11... | collective-permute-start | bytes 1966088 | tf_op jit(solution)/shard_map/ppermute | solution.py:466
  21.2 20.8 %all-to-all-start = ((f32[32,40,128]{2,1,0:T(8,128)}), f32[32,40,128]{2,1,0:T(8,128)S(1)}, u32[]{:S(2)}, u32[]{:S(2)}) async-start(f32[32,40,128]{2,1,0:T(8,128)} %bitcast.1), calls=%async_computation | async-start | bytes 1310720 | tf_op jit(solution)/shard_map/all_to_all | solution.py:453
  26.5 1.2 copy-start.4
  83.1 62.8 %all-to-all-start.1 = ((bf16[16,64,896]{2,1,0:T(8,128)(2,1)}), bf16[16,64,896]{2,1,0:T(8,128)(2,1)S(1)}, u32[]{:S(2)}, u32[]{:S(2)}) async-start(bf16[16,64,896]{2,1,0:T(8,128)(2,1)} %bitcast.14), calls=%async_computation.1 | async-start | bytes 3670016 | tf_op jit(solution)/shard_map/all_to_all | solution.py:453
  94.5 7.4 %collective-permute-start.1 = (f32[320,128]{1,0:T(8,128)S(1)}, f32[320,128]{1,0:T(8,128)S(1)}, u32[]{:S(2)}, u32[]{:S(2)}) collective-permute-start(f32[320,128]{1,0:T(8,128)S(1)} %bitcast.19), channel_id=1, source_target_pairs={{0,256},{256,0},{512,768},{768,512},{1,257},{257,1},{513,769},{769... | collective-permute-start | bytes 491528 | tf_op jit(solution)/shard_map/ppermute | solution.py:478
  102.0 11.3 %collective-permute-start.2 = (f32[640,128]{1,0:T(8,128)S(1)}, f32[640,128]{1,0:T(8,128)S(1)}, u32[]{:S(2)}, u32[]{:S(2)}) collective-permute-start(f32[640,128]{1,0:T(8,128)S(1)} %pad_maximum_fusion.near_ref), channel_id=1, source_target_pairs={{0,768},{256,512},{512,256},{768,0},{1,769},{257,513},{513,257},{7... | collective-permute-start | bytes 983048 | tf_op jit(solution)/shard_map/ppermute | solution.py:480
  105.5 11.8 %collective-permute-start.3 = (f32[640,128]{1,0:T(8,128)S(1)}, f32[640,128]{1,0:T(8,128)S(1)}, u32[]{:S(2)}, u32[]{:S(2)}) collective-permute-start(f32[640,128]{1,0:T(8,128)S(1)} %pad_maximum_fusion.near_ref), channel_id=1, source_target_pairs={{0,1},{1,0},{2,3},{3,2},{4,5},{5,4},{6,7},{7,6},{8,9},{9,8},{10,11... | collective-permute-start | bytes 983048 | tf_op jit(solution)/shard_map/ppermute | solution.py:481
  113.3 5.1 %collective-permute-start.4 = (f32[640,128]{1,0:T(8,128)S(1)}, f32[640,128]{1,0:T(8,128)S(1)}, u32[]{:S(2)}, u32[]{:S(2)}) collective-permute-start(f32[640,128]{1,0:T(8,128)S(1)} %collective-permute-done.2.far_ref), channel_id=1, source_target_pairs={{0,1},{1,0},{2,3},{3,2},{4,5},{5,4},{6,7},{7,6},{8,9},{9,8},{10,11... | collective-permute-start | bytes 983048 | tf_op jit(solution)/shard_map/ppermute | solution.py:482
  144.5 1.4 copy-start.2
  145.9 1.7 copy-start.3

commit v2 on v1

--- a/solution.py
+++ b/solution.py
@@ -18,13 +18,14 @@
 PAIRED = [(i, i + 2) for i in range(0, NBLK, 4)]
 TILES = len(WHOLE) + len(PAIRED) + 1
 HALF = TILES // 2 * BLK
-QUARTER = HALF // 4
+PART = HALF // 2
 WIDE = FEAT + LANES
 CAP = 64
 CL_OWN = 8
 INDEX_SPAN = 2**19
 PIECES = 2
-DEEP = 16
+AXES = ("x_hi", "x_lo", "z_hi", "z_lo", "y", "core")
+GROUP_SPLIT = (2, 2, 8, 2)
 HIGHEST = lax.Precision.HIGHEST
 VM = pl.BlockSpec(memory_space=pltpu.VMEM)
 SM = pl.BlockSpec(memory_space=pltpu.SMEM)
@@ -223,21 +224,15 @@
 def factor_kernel(
     total_rows, place_ref, near_ref, far_ref, near2_ref, far2_ref, out_ref, mean_ref, tri_ref, s_ref, w_ref, spot_ref, sems
 ):
-    core, column = place_ref[0], place_ref[1]
+    core, half = place_ref[0], place_ref[1]
     copies = []
     for side, parts in ((core, (near_ref, far_ref)), (1 - core, (near2_ref, far2_ref))):
-        spot = 0
-        for part in parts:
-            for at in range(0, part.shape[0], QUARTER):
-                piece = column ^ (spot ^ (spot >> 1))
-                copies.append(
-                    pltpu.make_async_copy(
-                        part.at[at : at + QUARTER],
-                        tri_ref.at[side, pl.ds(pl.multiple_of(piece * QUARTER, QUARTER), QUARTER)],
-                        sems.at[len(copies)],
-                    )
+        for part, spot in zip(parts, (half, 1 - half)):
+            copies.append(
+                pltpu.make_async_copy(
+                    part, tri_ref.at[side, pl.ds(pl.multiple_of(spot * PART, PART), PART)], sems.at[len(copies)]
                 )
-                spot += 1
+            )
     for copy in copies:
         copy.start()
     for copy in copies:
@@ -399,7 +394,7 @@
             pltpu.VMEM((FEAT, FEAT), F32),
             pltpu.VMEM((FEAT, FEAT), F32),
             pltpu.VMEM((128, LANES), F32),
-            pltpu.SemaphoreType.DMA((8,)),
+            pltpu.SemaphoreType.DMA((4,)),
         ],
         compiler_params=PARAMS,
         name="factor",
@@ -453,34 +448,46 @@
     return lax.all_to_all(x, axis, split_axis=0, concat_axis=0, tiled=True)
 
 
+def sum_parts(x, count):
+    share = x.size // (count * LANES)
+    if count % 2 == 0:
+        x = jnp.sum(x.reshape(count // 2, 2 * share, LANES), axis=0)
+        count = 2
+    return jnp.sum(x.reshape(count, share, LANES), axis=0)
+
+
+def copies_of(x, count):
+    return jnp.broadcast_to(x[None, :, None, :], (count, x.shape[0], 1, LANES))
+
+
 def on_device(embeddings, cluster_id, row_index):
     count = embeddings.shape[0]
-    across, deep, highs = lax.axis_size("x"), lax.axis_size("z"), lax.axis_size("y")
-    owners = 2 * highs
-    total_rows = count * owners * across * deep
-    shard, plane = ("y", "core"), ("x", "y")
+    size = {axis: lax.axis_size(axis) for axis in AXES}
+    owners = size["y"] * size["core"]
+    total_rows = count
+    for axis in AXES:
+        total_rows = total_rows * size[axis]
+    shard, plane = ("y", "core"), ("x_hi", "x_lo", "z_lo", "y")
     swap = [(0, 1), (1, 0)]
     core = lax.axis_index("core").astype(jnp.int32)
-    column = lax.axis_index("x").astype(jnp.int32)
+    half = lax.axis_index("x_hi").astype(jnp.int32)
     keep, send = moments(core.reshape(1), embeddings)
     pair = keep + lax.ppermute(send, "core", swap)
-    shares = across * highs
-    share = HALF // shares
+    near_shares = size["x_lo"] * size["z_lo"] * size["y"]
+    shares = size["x_hi"] * near_shares
     pair, embeddings = lax.optimization_barrier((pair, embeddings))
-    spread = exchange(pair.reshape(shares, share, LANES), plane)
+    spread = exchange(pair.reshape(shares, HALF // shares, 1, LANES), plane)
     packed, slot = pack(embeddings, cluster_id, row_index, owners)
-    part = jnp.sum(spread, axis=0)
+    part = sum_parts(spread, shares)
     part, packed = lax.optimization_barrier((part, packed))
-    total = jnp.sum(exchange(jnp.broadcast_to(part[None], (deep, share, LANES)), "z"), axis=0)
-    quarter = exchange(jnp.broadcast_to(total[None], (highs, share, LANES)), "y")
-    quarter = quarter.reshape(highs * share, LANES)
+    total = sum_parts(exchange(copies_of(part, size["z_hi"]), "z_hi"), size["z_hi"])
+    near = exchange(copies_of(total, near_shares), plane[1:]).reshape(PART, LANES)
     rows = exchange(packed.reshape(owners, CAP, WIDE), shard).reshape(owners * CAP, WIDE)
-    beside = lax.ppermute(quarter, "x", [(i, i ^ 1) for i in range(across)])
-    near = jnp.concatenate([quarter, beside], axis=0)
-    far = lax.ppermute(near, "x", [(i, i ^ 3) for i in range(across)])
+    columns = size["x_hi"] * size["x_lo"]
+    far = lax.ppermute(near, plane[:2], [(i, columns - 1 - i) for i in range(columns)])
     near2 = lax.ppermute(near, "core", swap)
     far2 = lax.ppermute(far, "core", swap)
-    place = jnp.stack([core, column])
+    place = jnp.stack([core, half])
     inverse, mean = factor(place, (near, far, near2, far2), total_rows)
     best = best_of(rows, inverse, mean)
     returned = exchange(best, shard)
@@ -488,16 +495,11 @@
 
 
 def solution(mesh):
-    groups, shards = mesh.devices.shape
-    deep = min(DEEP, groups)
-    split = Mesh(
-        mesh.devices.reshape(groups // deep, deep, shards // 2, 2), ("x", "z", "y", "core")
-    )
-    rows = ("x", "z", "y", "core")
+    split = Mesh(mesh.devices.reshape(GROUP_SPLIT + (-1, 2)), AXES)
     return jax.shard_map(
         on_device,
         mesh=split,
-        in_specs=(P(rows, None), P(rows), P(rows)),
-        out_specs=P(rows),
+        in_specs=(P(AXES, None), P(AXES), P(AXES)),
+        out_specs=P(AXES),
         check_vma=False,
     )

time: 171 us -> 160 us (0.936)
  starting transfers between devices: 44.4 us -> 37.1 us
  blocking collectives: 54.9 us -> 52.7 us
    all_to_all x2, waiting for transfers between devices: 14.2 us -> 17.7 us  [exchange(): return lax.all_to_all(x, axis, split_axis=0, concat_axis=0, tiled=True)]
    ppermute x2 -> x1, waiting for transfers between devices: 9.69 us -> 6.75 us  [on_device(): lax.ppermute(near, plane[:2], [(i, columns - 1 - i) for i in range(column...]
    all_to_all x2, starting transfers between devices: 15.3 us -> 12.5 us  [exchange(): return lax.all_to_all(x, axis, split_axis=0, concat_axis=0, tiled=True)]
    ppermute x2 -> x1, starting transfers between devices: 5.76 us -> 2.99 us  [on_device(): lax.ppermute(near, plane[:2], [(i, columns - 1 - i) for i in range(column...]
    all_to_all x3, blocking collectives: 54.9 us -> 52.7 us  [exchange(): return lax.all_to_all(x, axis, split_axis=0, concat_axis=0, tiled=True)]
  transfers between devices with their start and end apart: 7 -> 6, of which waited for: 5 -> 5; matrix products, arithmetic and copies ran while one was open for 0% -> 0% of each run, Pallas kernels for 16% -> 16%
where the time goes in v2:
time: 160 us
  blocking collectives  52.7 us (33%)
  starting transfers between devices  37.1 us (23%)
  Pallas kernels  35.8 us (22%)
  waiting for transfers between devices  27.3 us (17%)
  local copies, waits for them, and re-layouts  5.66 us (4%)
    all_to_all x3, blocking collectives, exchange(): return lax.all_to_all(x, axis, split_axis=0, concat_axis=0, tiled=True)  52.7 us
    pallas_call x1, Pallas kernels, factor(): pl.pallas_call(functools.partial(factor_kernel, total_rows), out_shape=(j...  24.8 us
    all_to_all x2, waiting for transfers between devices, exchange(): return lax.all_to_all(x, axis, split_axis=0, concat_axis=0, tiled=True)  17.7 us
    ppermute x1, starting transfers between devices, on_device(): pair = keep + lax.ppermute(send, 'core', swap)  16.2 us
    all_to_all x2, starting transfers between devices, exchange(): return lax.all_to_all(x, axis, split_axis=0, concat_axis=0, tiled=True)  12.5 us
    pallas_call x1, Pallas kernels, best_of(): pl.pallas_call(best_kernel, out_shape=jax.ShapeDtypeStruct((slots // CAP,...  7.61 us
    ppermute x1, waiting for transfers between devices, on_device(): lax.ppermute(near, plane[:2], [(i, columns - 1 - i) for i in range(column...  6.75 us
    unnamed x14, local copies, waits for them, and re-layouts  5.44 us
  transfers between devices with their start and end apart: 6, of which 5 were waited for; matrix products, arithmetic and copies ran while one was open for 0% of the time, Pallas kernels for 16%

profile of v2, /device:TPU:1, one launch (start us, length us, event | category | flops | bytes accessed | tf_op | source)
XLA Modules:
  0.0 159.8 jit_solution(13736943687790472047)
XLA Ops:
  0.0 0.0 copy-start
  0.0 1.1 copy-done
  1.1 1.2 moments.1
  2.3 0.0 copy-start.1
  2.3 0.0 copy-start.5
  2.3 0.0 copy-start.6
  2.3 16.2 %collective-permute-start = (f32[1280,128]{1,0:T(8,128)S(1)}, f32[1280,128]{1,0:T(8,128)S(1)}, u32[]{:S(2)}, u32[]{:S(2)}) collective-permute-start(f32[1280,128]{1,0:T(8,128)S(1)} %get-tuple-element.16), channel_id=1, source_target_pairs={{0,1},{1,0},{2,3},{3,2},{4,5},{5,4},{6,7},{7,6},{8,9},{9,8},{10,11... | collective-permute-start | bytes 1966088 | tf_op jit(solution)/shard_map/ppermute | solution.py:475
  18.5 1.7 %collective-permute-done = f32[1280,128]{1,0:T(8,128)S(1)} collective-permute-done((f32[1280,128]{1,0:T(8,128)S(1)}, f32[1280,128]{1,0:T(8,128)S(1)}, u32[]{:S(2)}, u32[]{:S(2)}) %collective-permute-start) | collective-permute-done | bytes 655392 | tf_op jit(solution)/shard_map/ppermute | solution.py:475
  20.2 0.9 add.3
  21.2 4.6 %all-to-all-start = ((f32[64,20,1,128]{3,2,1,0:T(1,128)}), f32[64,20,1,128]{3,2,1,0:T(1,128)S(1)}, u32[]{:S(2)}, u32[]{:S(2)}) async-start(f32[64,20,1,128]{3,2,1,0:T(1,128)} %bitcast.1), calls=%async_computation | async-start | bytes 1310720 | tf_op jit(solution)/shard_map/all_to_all | solution.py:448
  25.8 0.0 copy-done.1
  25.8 0.0 copy-done.5
  25.8 0.0 copy-done.6
  25.8 1.4 pack_rows.1
  27.3 0.0 copy-start.4
  27.3 1.2 copy-done.4
  28.5 16.6 %all-to-all-done = f32[64,20,1,128]{3,2,1,0:T(1,128)S(1)} async-done(((f32[64,20,1,128]{3,2,1,0:T(1,128)}), f32[64,20,1,128]{3,2,1,0:T(1,128)S(1)}, u32[]{:S(2)}, u32[]{:S(2)}) %all-to-all-start) | async-done | bytes 655392 | tf_op jit(solution)/shard_map/all_to_all | solution.py:448
  45.1 0.1 reduce_sum.36
  45.2 23.9 %all_to_all.31 = f32[8,20,1,128]{3,2,1,0:T(1,128)S(1)} all-to-all(f32[8,20,1,128]{3,2,1,0:T(1,128)S(1)} %broadcast_in_dim.4), channel_id=1, replica_groups=mesh['x_hi'=2,'x_lo'=2,'z_hi'=8,'z_lo'=2,'y'=8,'core'=2] {'z_hi'}, dimensions={0} | all-to-all | bytes 163840 | tf_op jit(solution)/shard_map/all_to_all | solution.py:448
  69.1 0.2 broadcast_in_dim.5
  69.3 15.9 %all_to_all.32 = f32[32,20,1,128]{3,2,1,0:T(1,128)S(1)} all-to-all(f32[32,20,1,128]{3,2,1,0:T(1,128)S(1)} %broadcast_in_dim.5), channel_id=1, replica_groups=mesh['x_hi'=2,'x_lo'=2,'z_hi'=8,'z_lo'=2,'y'=8,'core'=2] {'x_lo','z_lo',..., dimensions={0} | all-to-all | bytes 655360 | tf_op jit(solution)/shard_map/all_to_all | solution.py:448
  85.2 7.9 %all-to-all-start.1 = ((bf16[16,64,896]{2,1,0:T(8,128)(2,1)}), bf16[16,64,896]{2,1,0:T(8,128)(2,1)S(1)}, u32[]{:S(2)}, u32[]{:S(2)}) async-start(bf16[16,64,896]{2,1,0:T(8,128)(2,1)} %bitcast.16), calls=%async_computation.1 | async-start | bytes 3670016 | tf_op jit(solution)/shard_map/all_to_all | solution.py:448
  93.1 3.0 %collective-permute-start.1 = (f32[640,128]{1,0:T(8,128)S(1)}, f32[640,128]{1,0:T(8,128)S(1)}, u32[]{:S(2)}, u32[]{:S(2)}) collective-permute-start(f32[640,128]{1,0:T(8,128)S(1)} %bitcast.17), channel_id=1, source_target_pairs={{0,768},{256,512},{512,256},{768,0},{1,769},{257,513},{513,257},{7... | collective-permute-start | bytes 983048 | tf_op jit(solution)/shard_map/ppermute | solution.py:487
  96.1 2.4 %collective-permute-start.2 = (f32[640,128]{1,0:T(8,128)S(1)}, f32[640,128]{1,0:T(8,128)S(1)}, u32[]{:S(2)}, u32[]{:S(2)}) collective-permute-start(f32[640,128]{1,0:T(8,128)S(1)} %bitcast.18), channel_id=1, source_target_pairs={{0,1},{1,0},{2,3},{3,2},{4,5},{5,4},{6,7},{7,6},{8,9},{9,8},{10,11... | collective-permute-start | bytes 983048 | tf_op jit(solution)/shard_map/ppermute | solution.py:488
  98.5 6.7 %collective-permute-done.1.far_ref = f32[640,128]{1,0:T(8,128)S(1)} collective-permute-done((f32[640,128]{1,0:T(8,128)S(1)}, f32[640,128]{1,0:T(8,128)S(1)}, u32[]{:S(2)}, u32[]{:S(2)}) %collective-permute-start.1) | collective-permute-done | bytes 327712 | tf_op jit(solution)/shard_map/ppermute | solution.py:487
  105.2 2.9 %collective-permute-start.3 = (f32[640,128]{1,0:T(8,128)S(1)}, f32[640,128]{1,0:T(8,128)S(1)}, u32[]{:S(2)}, u32[]{:S(2)}) collective-permute-start(f32[640,128]{1,0:T(8,128)S(1)} %collective-permute-done.1.far_ref), channel_id=1, source_target_pairs={{0,1},{1,0},{2,3},{3,2},{4,5},{5,4},{6,7},{7,6},{8,9},{9,8},{10,11... | collective-permute-start | bytes 983048 | tf_op jit(solution)/shard_map/ppermute | solution.py:489
  108.2 0.1 pad_add_fusion.place_ref
  108.3 0.0 collective-permute-done.2.near2_ref
  108.3 1.2 collective-permute-done.3.far2_ref
  109.4 24.8 %factor.1 = (f32[768,768]{1,0:T(8,128)S(1)}, bf16[16,768]{1,0:T(8,128)(2,1)S(1)}) custom-call(s32[2]{0:T(128)S(1)} %pad_add_fusion.place_ref, f32[640,128]{1,0:T(8,128)S(1)} %bitcast.19, f32[640,128]{1,0:T(8,128)S(1)} %collective-permute-done.1.far_ref, f32[640,128]{1,0:T(8,128)S(1)} %collective-permute-done.2.near2_ref, ...), custom_call_target="tpu_custom_call" | custom-call | tf_op jit(solution)/shard_map/factor/pallas_call | solution.py:384
  134.2 0.0 copy-start.2
  134.3 1.4 copy-done.2
  135.7 1.1 all-to-all-done.1
  136.8 0.0 copy-start.3
  136.8 1.7 %copy-done.3 = f32[768,768]{1,0:T(8,128)S(1)} copy-done((f32[768,768]{1,0:T(8,128)S(1)}, f32[768,768]{1,0:T(8,128)}, u32[]{:S(2)}) %copy-start.3) | copy-done | bytes 2359320
  138.4 7.6 %best.1 = f32[16,64]{1,0:T(8,128)S(1)} custom-call(bf16[1024,896]{1,0:T(8,128)(2,1)S(1)} %bitcast.15, f32[768,768]{1,0:T(8,128)S(1)} %copy-done.3, bf16[16,768]{1,0:T(8,128)(2,1)S(1)} %get-tuple-element.23.mean_ref), custom_call_target="tpu_custom_call" | custom-call | tf_op jit(solution)/shard_map/best/pallas_call | solution.py:406
  146.1 13.0 %all_to_all.33 = f32[16,1,64]{2,1,0:T(1,128)S(1)} all-to-all(f32[16,1,64]{2,1,0:T(1,128)S(1)} %bitcast.20), channel_id=1, replica_groups=mesh['x_hi'=2,'x_lo'=2,'z_hi'=8,'z_lo'=2,'y'=8,'core'=2] {'y','core'}, dimensions={0} | all-to-all | bytes 8192 | tf_op jit(solution)/shard_map/all_to_all | solution.py:448
  159.0 0.8 unpack.1
  (6 shorter events, 0.1 us)
Async XLA Ops:
  0.0 1.1 copy-start
  2.3 23.5 %copy-start.1 = (bf16[512,768]{1,0:T(8,128)(2,1)S(1)}, bf16[512,768]{1,0:T(8,128)(2,1)}, u32[]{:S(2)}) copy-start(bf16[512,768]{1,0:T(8,128)(2,1)} %x_ref.2) | copy-start | bytes 2359300
  2.3 23.5 %copy-start.5 = (s32[512]{0:T(512)S(1)}, s32[512]{0:T(512)}, u32[]{:S(2)}) copy-start(s32[512]{0:T(512)} %param.4) | copy-start | bytes 6148
  2.3 23.5 %copy-start.6 = (s32[512]{0:T(512)S(1)}, s32[512]{0:T(512)}, u32[]{:S(2)}) copy-start(s32[512]{0:T(512)} %param.5) | copy-start | bytes 6148
  2.3 17.9 %collective-permute-start = (f32[1280,128]{1,0:T(8,128)S(1)}, f32[1280,128]{1,0:T(8,128)S(1)}, u32[]{:S(2)}, u32[]{:S(2)}) collective-permute-start(f32[1280,128]{1,0:T(8,128)S(1)} %get-tuple-element.16), channel_id=1, source_target_pairs={{0,1},{1,0},{2,3},{3,2},{4,5},{5,4},{6,7},{7,6},{8,9},{9,8},{10,11... | collective-permute-start | bytes 1966088 | tf_op jit(solution)/shard_map/ppermute | solution.py:475
  21.2 23.9 %all-to-all-start = ((f32[64,20,1,128]{3,2,1,0:T(1,128)}), f32[64,20,1,128]{3,2,1,0:T(1,128)S(1)}, u32[]{:S(2)}, u32[]{:S(2)}) async-start(f32[64,20,1,128]{3,2,1,0:T(1,128)} %bitcast.1), calls=%async_computation | async-start | bytes 1310720 | tf_op jit(solution)/shard_map/all_to_all | solution.py:448
  27.3 1.2 copy-start.4
  85.2 51.6 %all-to-all-start.1 = ((bf16[16,64,896]{2,1,0:T(8,128)(2,1)}), bf16[16,64,896]{2,1,0:T(8,128)(2,1)S(1)}, u32[]{:S(2)}, u32[]{:S(2)}) async-start(bf16[16,64,896]{2,1,0:T(8,128)(2,1)} %bitcast.16), calls=%async_computation.1 | async-start | bytes 3670016 | tf_op jit(solution)/shard_map/all_to_all | solution.py:448
  93.1 12.2 %collective-permute-start.1 = (f32[640,128]{1,0:T(8,128)S(1)}, f32[640,128]{1,0:T(8,128)S(1)}, u32[]{:S(2)}, u32[]{:S(2)}) collective-permute-start(f32[640,128]{1,0:T(8,128)S(1)} %bitcast.17), channel_id=1, source_target_pairs={{0,768},{256,512},{512,256},{768,0},{1,769},{257,513},{513,257},{7... | collective-permute-start | bytes 983048 | tf_op jit(solution)/shard_map/ppermute | solution.py:487
  96.1 12.2 %collective-permute-start.2 = (f32[640,128]{1,0:T(8,128)S(1)}, f32[640,128]{1,0:T(8,128)S(1)}, u32[]{:S(2)}, u32[]{:S(2)}) collective-permute-start(f32[640,128]{1,0:T(8,128)S(1)} %bitcast.18), channel_id=1, source_target_pairs={{0,1},{1,0},{2,3},{3,2},{4,5},{5,4},{6,7},{7,6},{8,9},{9,8},{10,11... | collective-permute-start | bytes 983048 | tf_op jit(solution)/shard_map/ppermute | solution.py:488
  105.2 4.2 %collective-permute-start.3 = (f32[640,128]{1,0:T(8,128)S(1)}, f32[640,128]{1,0:T(8,128)S(1)}, u32[]{:S(2)}, u32[]{:S(2)}) collective-permute-start(f32[640,128]{1,0:T(8,128)S(1)} %collective-permute-done.1.far_ref), channel_id=1, source_target_pairs={{0,1},{1,0},{2,3},{3,2},{4,5},{5,4},{6,7},{7,6},{8,9},{9,8},{10,11... | collective-permute-start | bytes 983048 | tf_op jit(solution)/shard_map/ppermute | solution.py:489
  134.2 1.4 copy-start.2
  136.8 1.7 %copy-start.3 = (f32[768,768]{1,0:T(8,128)S(1)}, f32[768,768]{1,0:T(8,128)}, u32[]{:S(2)}) copy-start(f32[768,768]{1,0:T(8,128)} %copy-done.2) | copy-start | bytes 7077892

commit v3 on v2

--- a/solution.py
+++ b/solution.py
@@ -222,7 +222,7 @@
 
 
 def factor_kernel(
-    total_rows, place_ref, near_ref, far_ref, near2_ref, far2_ref, out_ref, mean_ref, tri_ref, s_ref, w_ref, spot_ref, sems
+    total_rows, place_ref, near_ref, far_ref, near2_ref, far2_ref, out_ref, mean_ref, tri_ref, s_ref, w_ref, leave_ref, spot_ref, sems
 ):
     core, half = place_ref[0], place_ref[1]
     copies = []
@@ -249,17 +249,41 @@
     def mean_column(i):
         return turned[BLK * (i % 2) : BLK * (i % 2 + 1), 8 * (i // 2) : 8 * (i // 2) + 1]
 
+    eye = lax.broadcasted_iota(jnp.int32, (BLK, BLK), 0) == lax.broadcasted_iota(
+        jnp.int32, (BLK, BLK), 1
+    )
+    blocks = []
+    for i in range(NBLK):
+        if i % 2:
+            both = get(WHOLE.index((i, i // 2)))[:, BLK:]
+            mean = means[i // 2][:, BLK:]
+        else:
+            n = [pair for pair in PAIRED if i in pair][0]
+            both = get(len(WHOLE) + PAIRED.index(n))
+            both = both[:, :BLK] if n[0] == i else both[:, BLK:]
+            mean = means[i // 2][:, :BLK]
+        blocks.append(both - mean_column(i) * mean)
+    variance = [jnp.sum(jnp.where(eye, block, 0.0), axis=0, keepdims=True) for block in blocks]
+    scale = [
+        lax.rsqrt(jnp.concatenate(variance[2 * j : 2 * j + 2], axis=1)) for j in range(FEAT // LANES)
+    ]
+    upright = jnp.concatenate(
+        [jnp.broadcast_to(part, (8, LANES)) for part in scale]
+        + [jnp.zeros((BLK - 8 * (FEAT // LANES), LANES), F32)],
+        axis=0,
+    ).T
+
+    def scale_column(i):
+        return upright[BLK * (i % 2) : BLK * (i % 2 + 1), 8 * (i // 2) : 8 * (i // 2) + 1]
+
     for tile, (i, j) in enumerate(WHOLE):
         s_ref[BLK * i : BLK * (i + 1), LANES * j : LANES * (j + 1)] = (
-            get(tile) - mean_column(i) * means[j]
+            (get(tile) - mean_column(i) * means[j]) * scale_column(i) * scale[j]
         )
-    for n, pair in enumerate(PAIRED):
-        both = get(len(WHOLE) + n)
-        for side, i in enumerate(pair):
-            part = both[:, BLK * side : BLK * (side + 1)]
-            s_ref[BLK * i : BLK * (i + 1), BLK * i : BLK * (i + 1)] = (
-                part - mean_column(i) * means[i // 2][:, :BLK]
-            )
+    for i in range(0, NBLK, 2):
+        s_ref[BLK * i : BLK * (i + 1), BLK * i : BLK * (i + 1)] = (
+            blocks[i] * scale_column(i) * scale[i // 2][:, :BLK]
+        )
     parts = split3(jnp.concatenate(means, axis=1))
     mean_ref[...] = jnp.concatenate(
         [p.astype(F32) for p in parts] + [jnp.zeros((13, FEAT), F32)], axis=0
@@ -298,8 +322,10 @@
             w_ref[at:to, :at] = nn(left6(inv), right6(w_ref[at:to, :at], 0))
         w_ref[at:to, at:to] = inv
         if to % 256 == 0:
+            wide = jnp.concatenate(scale, axis=1)
+            leave_ref[to - 256 : to, :to] = w_ref[to - 256 : to, :to] * wide[:, :to]
             copy = pltpu.make_async_copy(
-                w_ref.at[to - 256 : to, 0:to], out_ref.at[to - 256 : to, 0:to], sems.at[to // 256 - 1]
+                leave_ref.at[to - 256 : to, 0:to], out_ref.at[to - 256 : to, 0:to], sems.at[to // 256 - 1]
             )
             copy.start()
             leaving.append(copy)
@@ -307,29 +333,12 @@
         copy.wait()
 
 
-def best_kernel(rows_ref, inverse_ref, mean_ref, best_ref, w_ref, x_ref, z_ref, u_ref, sems):
-    slots = rows_ref.shape[0]
+def best_kernel(x_ref, inverse_ref, mean_ref, best_ref, z_ref, u_ref):
+    slots = x_ref.shape[0]
     piece = slots // PIECES
-    copies = [
-        pltpu.make_async_copy(
-            rows_ref.at[piece * i : piece * (i + 1)], x_ref.at[piece * i : piece * (i + 1)], sems.at[i]
-        )
-        for i in range(PIECES)
+    parts = [
+        split3(inverse_ref[256 * n : 256 * (n + 1), : 256 * (n + 1)]) for n in range(FEAT // 256)
     ]
-    fetch = [
-        pltpu.make_async_copy(
-            inverse_ref.at[256 * n : 256 * (n + 1), 0 : 256 * (n + 1)],
-            w_ref.at[256 * n : 256 * (n + 1), 0 : 256 * (n + 1)],
-            sems.at[PIECES + n],
-        )
-        for n in range(FEAT // 256)
-    ]
-    for copy in fetch + copies:
-        copy.start()
-    parts = []
-    for n in range(FEAT // 256):
-        fetch[n].wait()
-        parts.append(split3(w_ref[256 * n : 256 * (n + 1), : 256 * (n + 1)]))
 
     def whiten(x, n):
         high, mid, low = parts[n]
@@ -339,8 +348,7 @@
     shift = [
         jnp.sum(whiten(mean_ref[...], n), axis=0, keepdims=True) for n in range(FEAT // 256)
     ]
-    for i, copy in enumerate(copies):
-        copy.wait()
+    for i in range(PIECES):
         here = slice(piece * i, piece * (i + 1))
         x = x_ref[here, :FEAT]
         norm = jnp.zeros((piece, 1), F32)
@@ -393,6 +401,7 @@
             pltpu.VMEM((2, HALF, LANES), F32),
             pltpu.VMEM((FEAT, FEAT), F32),
             pltpu.VMEM((FEAT, FEAT), F32),
+            pltpu.VMEM((FEAT, FEAT), F32),
             pltpu.VMEM((128, LANES), F32),
             pltpu.SemaphoreType.DMA((4,)),
         ],
@@ -406,15 +415,9 @@
     return pl.pallas_call(
         best_kernel,
         out_shape=jax.ShapeDtypeStruct((slots // CAP, CAP), F32),
-        in_specs=[HBM, HBM, VM],
+        in_specs=[VM, VM, VM],
         out_specs=VM,
-        scratch_shapes=[
-            pltpu.VMEM((FEAT, FEAT), F32),
-            pltpu.VMEM((slots, WIDE), BF16),
-            pltpu.VMEM((slots, FEAT), F32),
-            pltpu.VMEM((slots, FEAT), BF16),
-            pltpu.SemaphoreType.DMA((PIECES + FEAT // 256,)),
-        ],
+        scratch_shapes=[pltpu.VMEM((slots, FEAT), F32), pltpu.VMEM((slots, FEAT), BF16)],
         compiler_params=PARAMS,
         name="best",
     )(rows, inverse, mean)

time: 160 us -> 159 us (level)
    pallas_call x1, Pallas kernels: 7.61 us -> 5.43 us  [best_of(): pl.pallas_call(best_kernel, out_shape=jax.ShapeDtypeStruct((slots // CAP,...]
  transfers between devices with their start and end apart: 6 -> 6, of which waited for: 5 -> 5; matrix products, arithmetic and copies ran while one was open for 0% -> 0% of each run, Pallas kernels for 16% -> 17%
where the time goes in v3:
time: 159 us; the launch traced here: 158 us
  blocking collectives  53.4 us (34%)
  starting transfers between devices  37.1 us (23%)
  Pallas kernels  34.3 us (22%)
  waiting for transfers between devices  26.6 us (17%)
  local copies, waits for them, and re-layouts  5.66 us (4%)
    all_to_all x3, blocking collectives, exchange(): return lax.all_to_all(x, axis, split_axis=0, concat_axis=0, tiled=True)  53.4 us
    pallas_call x1, Pallas kernels, factor(): pl.pallas_call(functools.partial(factor_kernel, total_rows), out_shape=(j...  25.5 us
    all_to_all x2, waiting for transfers between devices, exchange(): return lax.all_to_all(x, axis, split_axis=0, concat_axis=0, tiled=True)  17 us
    ppermute x1, starting transfers between devices, on_device(): pair = keep + lax.ppermute(send, 'core', swap)  16.2 us
    all_to_all x2, starting transfers between devices, exchange(): return lax.all_to_all(x, axis, split_axis=0, concat_axis=0, tiled=True)  12.5 us
    ppermute x1, waiting for transfers between devices, on_device(): lax.ppermute(near, plane[:2], [(i, columns - 1 - i) for i in range(column...  6.75 us
    unnamed x14, local copies, waits for them, and re-layouts  5.44 us
    pallas_call x1, Pallas kernels, best_of(): pl.pallas_call(best_kernel, out_shape=jax.ShapeDtypeStruct((slots // CAP,...  5.43 us
  transfers between devices with their start and end apart: 6, of which 5 were waited for; matrix products, arithmetic and copies ran while one was open for 0% of the time, Pallas kernels for 17%

profile of v3, /device:TPU:1, one launch (start us, length us, event | category | flops | bytes accessed | tf_op | source)
XLA Modules:
  0.0 158.3 jit_solution(9012428136982825503)
XLA Ops:
  0.0 0.0 copy-start
  0.0 1.1 copy-done
  1.1 1.2 moments.1
  2.3 0.0 copy-start.1
  2.3 0.0 copy-start.5
  2.3 0.0 copy-start.6
  2.3 16.2 %collective-permute-start = (f32[1280,128]{1,0:T(8,128)S(1)}, f32[1280,128]{1,0:T(8,128)S(1)}, u32[]{:S(2)}, u32[]{:S(2)}) collective-permute-start(f32[1280,128]{1,0:T(8,128)S(1)} %get-tuple-element.16), channel_id=1, source_target_pairs={{0,1},{1,0},{2,3},{3,2},{4,5},{5,4},{6,7},{7,6},{8,9},{9,8},{10,11... | collective-permute-start | bytes 1966088 | tf_op jit(solution)/shard_map/ppermute | solution.py:478
  18.5 1.7 %collective-permute-done = f32[1280,128]{1,0:T(8,128)S(1)} collective-permute-done((f32[1280,128]{1,0:T(8,128)S(1)}, f32[1280,128]{1,0:T(8,128)S(1)}, u32[]{:S(2)}, u32[]{:S(2)}) %collective-permute-start) | collective-permute-done | bytes 655392 | tf_op jit(solution)/shard_map/ppermute | solution.py:478
  20.2 0.9 add.3
  21.2 4.6 %all-to-all-start = ((f32[64,20,1,128]{3,2,1,0:T(1,128)}), f32[64,20,1,128]{3,2,1,0:T(1,128)S(1)}, u32[]{:S(2)}, u32[]{:S(2)}) async-start(f32[64,20,1,128]{3,2,1,0:T(1,128)} %bitcast.1), calls=%async_computation | async-start | bytes 1310720 | tf_op jit(solution)/shard_map/all_to_all | solution.py:451
  25.8 0.0 copy-done.1
  25.8 0.0 copy-done.5
  25.8 0.0 copy-done.6
  25.8 1.4 pack_rows.1
  27.3 0.0 copy-start.4
  27.3 1.2 copy-done.4
  28.5 16.6 %all-to-all-done = f32[64,20,1,128]{3,2,1,0:T(1,128)S(1)} async-done(((f32[64,20,1,128]{3,2,1,0:T(1,128)}), f32[64,20,1,128]{3,2,1,0:T(1,128)S(1)}, u32[]{:S(2)}, u32[]{:S(2)}) %all-to-all-start) | async-done | bytes 655392 | tf_op jit(solution)/shard_map/all_to_all | solution.py:451
  45.1 0.1 reduce_sum.36
  45.2 23.9 %all_to_all.31 = f32[8,20,1,128]{3,2,1,0:T(1,128)S(1)} all-to-all(f32[8,20,1,128]{3,2,1,0:T(1,128)S(1)} %broadcast_in_dim.4), channel_id=1, replica_groups=mesh['x_hi'=2,'x_lo'=2,'z_hi'=8,'z_lo'=2,'y'=8,'core'=2] {'z_hi'}, dimensions={0} | all-to-all | bytes 163840 | tf_op jit(solution)/shard_map/all_to_all | solution.py:451
  69.1 0.2 broadcast_in_dim.5
  69.3 15.9 %all_to_all.32 = f32[32,20,1,128]{3,2,1,0:T(1,128)S(1)} all-to-all(f32[32,20,1,128]{3,2,1,0:T(1,128)S(1)} %broadcast_in_dim.5), channel_id=1, replica_groups=mesh['x_hi'=2,'x_lo'=2,'z_hi'=8,'z_lo'=2,'y'=8,'core'=2] {'x_lo','z_lo',..., dimensions={0} | all-to-all | bytes 655360 | tf_op jit(solution)/shard_map/all_to_all | solution.py:451
  85.2 7.9 %all-to-all-start.1 = ((bf16[16,64,896]{2,1,0:T(8,128)(2,1)}), bf16[16,64,896]{2,1,0:T(8,128)(2,1)S(1)}, u32[]{:S(2)}, u32[]{:S(2)}) async-start(bf16[16,64,896]{2,1,0:T(8,128)(2,1)} %bitcast.16), calls=%async_computation.1 | async-start | bytes 3670016 | tf_op jit(solution)/shard_map/all_to_all | solution.py:451
  93.1 3.0 %collective-permute-start.1 = (f32[640,128]{1,0:T(8,128)S(1)}, f32[640,128]{1,0:T(8,128)S(1)}, u32[]{:S(2)}, u32[]{:S(2)}) collective-permute-start(f32[640,128]{1,0:T(8,128)S(1)} %bitcast.17), channel_id=1, source_target_pairs={{0,768},{256,512},{512,256},{768,0},{1,769},{257,513},{513,257},{7... | collective-permute-start | bytes 983048 | tf_op jit(solution)/shard_map/ppermute | solution.py:490
  96.1 2.4 %collective-permute-start.2 = (f32[640,128]{1,0:T(8,128)S(1)}, f32[640,128]{1,0:T(8,128)S(1)}, u32[]{:S(2)}, u32[]{:S(2)}) collective-permute-start(f32[640,128]{1,0:T(8,128)S(1)} %bitcast.18), channel_id=1, source_target_pairs={{0,1},{1,0},{2,3},{3,2},{4,5},{5,4},{6,7},{7,6},{8,9},{9,8},{10,11... | collective-permute-start | bytes 983048 | tf_op jit(solution)/shard_map/ppermute | solution.py:491
  98.5 6.7 %collective-permute-done.1.far_ref = f32[640,128]{1,0:T(8,128)S(1)} collective-permute-done((f32[640,128]{1,0:T(8,128)S(1)}, f32[640,128]{1,0:T(8,128)S(1)}, u32[]{:S(2)}, u32[]{:S(2)}) %collective-permute-start.1) | collective-permute-done | bytes 327712 | tf_op jit(solution)/shard_map/ppermute | solution.py:490
  105.2 2.9 %collective-permute-start.3 = (f32[640,128]{1,0:T(8,128)S(1)}, f32[640,128]{1,0:T(8,128)S(1)}, u32[]{:S(2)}, u32[]{:S(2)}) collective-permute-start(f32[640,128]{1,0:T(8,128)S(1)} %collective-permute-done.1.far_ref), channel_id=1, source_target_pairs={{0,1},{1,0},{2,3},{3,2},{4,5},{5,4},{6,7},{7,6},{8,9},{9,8},{10,11... | collective-permute-start | bytes 983048 | tf_op jit(solution)/shard_map/ppermute | solution.py:492
  108.2 0.1 pad_add_fusion.place_ref
  108.3 0.0 collective-permute-done.2.near2_ref
  108.3 1.2 collective-permute-done.3.far2_ref
  109.4 25.5 %factor.1 = (f32[768,768]{1,0:T(8,128)S(1)}, bf16[16,768]{1,0:T(8,128)(2,1)S(1)}) custom-call(s32[2]{0:T(128)S(1)} %pad_add_fusion.place_ref, f32[640,128]{1,0:T(8,128)S(1)} %bitcast.19, f32[640,128]{1,0:T(8,128)S(1)} %collective-permute-done.1.far_ref, f32[640,128]{1,0:T(8,128)S(1)} %collective-permute-done.2.near2_ref, ...), custom_call_target="tpu_custom_call" | custom-call | tf_op jit(solution)/shard_map/factor/pallas_call | solution.py:392
  135.0 0.0 copy-start.2
  135.0 1.4 copy-done.2
  136.4 0.4 all-to-all-done.1
  136.8 0.0 copy-start.3
  136.8 1.7 %copy-done.3 = f32[768,768]{1,0:T(8,128)S(1)} copy-done((f32[768,768]{1,0:T(8,128)S(1)}, f32[768,768]{1,0:T(8,128)}, u32[]{:S(2)}) %copy-start.3) | copy-done | bytes 2359320
  138.4 5.4 %best.1 = f32[16,64]{1,0:T(8,128)S(1)} custom-call(bf16[1024,896]{1,0:T(8,128)(2,1)S(1)} %bitcast.15, f32[768,768]{1,0:T(8,128)S(1)} %copy-done.3, bf16[16,768]{1,0:T(8,128)(2,1)S(1)} %get-tuple-element.23.mean_ref), custom_call_target="tpu_custom_call" | custom-call | tf_op jit(solution)/shard_map/best/pallas_call | solution.py:415
  143.9 13.7 %all_to_all.33 = f32[16,1,64]{2,1,0:T(1,128)S(1)} all-to-all(f32[16,1,64]{2,1,0:T(1,128)S(1)} %bitcast.20), channel_id=1, replica_groups=mesh['x_hi'=2,'x_lo'=2,'z_hi'=8,'z_lo'=2,'y'=8,'core'=2] {'y','core'}, dimensions={0} | all-to-all | bytes 8192 | tf_op jit(solution)/shard_map/all_to_all | solution.py:451
  157.6 0.8 unpack.1
  (6 shorter events, 0.1 us)
Async XLA Ops:
  0.0 1.1 copy-start
  2.3 23.5 %copy-start.1 = (bf16[512,768]{1,0:T(8,128)(2,1)S(1)}, bf16[512,768]{1,0:T(8,128)(2,1)}, u32[]{:S(2)}) copy-start(bf16[512,768]{1,0:T(8,128)(2,1)} %x_ref.2) | copy-start | bytes 2359300
  2.3 23.5 %copy-start.5 = (s32[512]{0:T(512)S(1)}, s32[512]{0:T(512)}, u32[]{:S(2)}) copy-start(s32[512]{0:T(512)} %param.4) | copy-start | bytes 6148
  2.3 23.5 %copy-start.6 = (s32[512]{0:T(512)S(1)}, s32[512]{0:T(512)}, u32[]{:S(2)}) copy-start(s32[512]{0:T(512)} %param.5) | copy-start | bytes 6148
  2.3 17.9 %collective-permute-start = (f32[1280,128]{1,0:T(8,128)S(1)}, f32[1280,128]{1,0:T(8,128)S(1)}, u32[]{:S(2)}, u32[]{:S(2)}) collective-permute-start(f32[1280,128]{1,0:T(8,128)S(1)} %get-tuple-element.16), channel_id=1, source_target_pairs={{0,1},{1,0},{2,3},{3,2},{4,5},{5,4},{6,7},{7,6},{8,9},{9,8},{10,11... | collective-permute-start | bytes 1966088 | tf_op jit(solution)/shard_map/ppermute | solution.py:478
  21.2 23.9 %all-to-all-start = ((f32[64,20,1,128]{3,2,1,0:T(1,128)}), f32[64,20,1,128]{3,2,1,0:T(1,128)S(1)}, u32[]{:S(2)}, u32[]{:S(2)}) async-start(f32[64,20,1,128]{3,2,1,0:T(1,128)} %bitcast.1), calls=%async_computation | async-start | bytes 1310720 | tf_op jit(solution)/shard_map/all_to_all | solution.py:451
  27.3 1.2 copy-start.4
  85.2 51.6 %all-to-all-start.1 = ((bf16[16,64,896]{2,1,0:T(8,128)(2,1)}), bf16[16,64,896]{2,1,0:T(8,128)(2,1)S(1)}, u32[]{:S(2)}, u32[]{:S(2)}) async-start(bf16[16,64,896]{2,1,0:T(8,128)(2,1)} %bitcast.16), calls=%async_computation.1 | async-start | bytes 3670016 | tf_op jit(solution)/shard_map/all_to_all | solution.py:451
  93.1 12.2 %collective-permute-start.1 = (f32[640,128]{1,0:T(8,128)S(1)}, f32[640,128]{1,0:T(8,128)S(1)}, u32[]{:S(2)}, u32[]{:S(2)}) collective-permute-start(f32[640,128]{1,0:T(8,128)S(1)} %bitcast.17), channel_id=1, source_target_pairs={{0,768},{256,512},{512,256},{768,0},{1,769},{257,513},{513,257},{7... | collective-permute-start | bytes 983048 | tf_op jit(solution)/shard_map/ppermute | solution.py:490
  96.1 12.2 %collective-permute-start.2 = (f32[640,128]{1,0:T(8,128)S(1)}, f32[640,128]{1,0:T(8,128)S(1)}, u32[]{:S(2)}, u32[]{:S(2)}) collective-permute-start(f32[640,128]{1,0:T(8,128)S(1)} %bitcast.18), channel_id=1, source_target_pairs={{0,1},{1,0},{2,3},{3,2},{4,5},{5,4},{6,7},{7,6},{8,9},{9,8},{10,11... | collective-permute-start | bytes 983048 | tf_op jit(solution)/shard_map/ppermute | solution.py:491
  105.2 4.2 %collective-permute-start.3 = (f32[640,128]{1,0:T(8,128)S(1)}, f32[640,128]{1,0:T(8,128)S(1)}, u32[]{:S(2)}, u32[]{:S(2)}) collective-permute-start(f32[640,128]{1,0:T(8,128)S(1)} %collective-permute-done.1.far_ref), channel_id=1, source_target_pairs={{0,1},{1,0},{2,3},{3,2},{4,5},{5,4},{6,7},{7,6},{8,9},{9,8},{10,11... | collective-permute-start | bytes 983048 | tf_op jit(solution)/shard_map/ppermute | solution.py:492
  135.0 1.4 copy-start.2
  136.8 1.7 %copy-start.3 = (f32[768,768]{1,0:T(8,128)S(1)}, f32[768,768]{1,0:T(8,128)}, u32[]{:S(2)}) copy-start(f32[768,768]{1,0:T(8,128)} %copy-done.2) | copy-start | bytes 7077892
